TPU v7x, 32 devices: a whole 2x2x4 slice. The times are simulated.
32 devices in a mesh: dp: 8 (over z, x), ctx: 4 (over y, core).
Axes of the slice: x: 2, y: 2, z: 4, core: 2. Of those that a mesh axis runs over, the one named last changes fastest.
Arguments:
- block_input: bfloat16 [8, 2048, 2048], P('dp', 'ctx'), may hold values from -6 to 6
- segment_ids: int32 [8, 2048], P('dp', 'ctx'), may hold values from 0 to 5, never falling along the last dimension, each value on 1 to 800 neighbouring positions
- cotangent: bfloat16 [8, 2048, 2048], P('dp', 'ctx'), may hold values from -6 to 6
- in_weight: float32 [2048, 8240], P(('dp', 'ctx')), may hold values from -0.125 to 0.125
- out_weight: float32 [4096, 2048], P(('dp', 'ctx')), may hold values from -0.375 to 0.375
- gate_up_weight: float32 [2048, 8192], P(('dp', 'ctx')), may hold values from -0.125 to 0.125
- down_weight: float32 [4096, 2048], P(('dp', 'ctx')), may hold values from -0.09375 to 0.09375
- in_first: float32 [2048, 8240], P(('dp', 'ctx')), may hold values from -40 to 40
- out_first: float32 [4096, 2048], P(('dp', 'ctx')), may hold values from -40 to 40
- gate_up_first: float32 [2048, 8192], P(('dp', 'ctx')), may hold values from -40 to 40
- down_first: float32 [4096, 2048], P(('dp', 'ctx')), may hold values from -40 to 40
- in_second: float32 [2048, 8240], P(('dp', 'ctx')), may hold values from 212.992 to 868.352
- out_second: float32 [4096, 2048], P(('dp', 'ctx')), may hold values from 212.992 to 868.352
- gate_up_second: float32 [2048, 8192], P(('dp', 'ctx')), may hold values from 212.992 to 868.352
- down_second: float32 [4096, 2048], P(('dp', 'ctx')), may hold values from 212.992 to 868.352
- small_params: float32 [7312], replicated, may hold values from -5 to 1.5
- small_first: float32 [7312], replicated, may hold values from -80 to 80
- small_second: float32 [7312], replicated, may hold values from 819.2 to 3276.8
Outputs:
- block_output: bfloat16 [8, 2048, 2048], P('dp', 'ctx')
- input_grad: float32 [8, 2048, 2048], P('dp', 'ctx')
- new_in_weight: float32 [2048, 8240], P(('dp', 'ctx'))
- new_in_first: float32 [2048, 8240], P(('dp', 'ctx'))
- new_in_second: float32 [2048, 8240], P(('dp', 'ctx'))
- new_out_weight: float32 [4096, 2048], P(('dp', 'ctx'))
- new_out_first: float32 [4096, 2048], P(('dp', 'ctx'))
- new_out_second: float32 [4096, 2048], P(('dp', 'ctx'))
- new_gate_up_weight: float32 [2048, 8192], P(('dp', 'ctx'))
- new_gate_up_first: float32 [2048, 8192], P(('dp', 'ctx'))
- new_gate_up_second: float32 [2048, 8192], P(('dp', 'ctx'))
- new_down_weight: float32 [4096, 2048], P(('dp', 'ctx'))
- new_down_first: float32 [4096, 2048], P(('dp', 'ctx'))
- new_down_second: float32 [4096, 2048], P(('dp', 'ctx'))
- new_small_params: float32 [7312], replicated
- new_small_first: float32 [7312], replicated
- new_small_second: float32 [7312], replicated
All inputs are finite; a program needn't handle non-finite values.
Results may differ from a plain program's by a relative error of at most 0.013.
The roundings to bfloat16 on the way count: a program that leaves them out, or rounds other values in their place, can miss the bound.
Values may be sent and summed in bfloat16 or wider, within the bound.
No kernel may reach another device: no remote copies, remote signals or barrier semaphores. Data moves between devices by JAX's collectives and lax.ppermute only.
A program may use at most 576 MiB of HBM per device.

v0:
```python
import math

import jax
import jax.numpy as jnp
from jax import lax
from jax.sharding import PartitionSpec as P

D = 2048
FF = 4096
QH = 8
KVH = 2
HD = 128
HEADS_M = 48
HEAD_M = 64
STATE = 256
STEP = 10


highest = lax.Precision.HIGHEST
norm_eps = 1e-05
beta_one = 0.9
beta_two = 0.95
adam_eps = 1e-08
weight_decay = 0.1
rate_scale = 3.0
small_rate = 0.3


def prefix(x, axis, combine, identity):
    devices, position = (lax.axis_size(axis), lax.axis_index(axis))
    everything = jax.tree.map(
        lambda part, kind: lax.all_gather(part.astype(kind), axis), x, (jnp.bfloat16, jnp.bfloat16)
    )
    start = jax.tree.map(
        lambda part, zero: jnp.broadcast_to(jnp.asarray(zero, part.dtype), part.shape), x, identity
    )

    def turn(k, before):
        reached = k < position
        new = combine(
            before, jax.tree.map(lambda part, own: part[k].astype(own.dtype), everything, x)
        )
        return jax.tree.map(lambda a, b: jnp.where(reached, a, b), new, before)

    return lax.fori_loop(0, devices, turn, start)


def carried_in(x, axis, join, neutral):
    count = lax.axis_size(axis)
    place = lax.axis_index(axis)
    ahead = count - 1 - place
    gathered = jax.tree.map(
        lambda a, kind: lax.all_gather(a.astype(kind), axis),
        x,
        jax.tree.map(lambda a: jnp.bfloat16 if a.dtype == jnp.float32 else a.dtype, x),
    )
    state = jax.tree.map(lambda a, e: jnp.zeros_like(a) + jnp.asarray(e, a.dtype), x, neutral)

    def one(turn, state):
        source = count - 1 - turn
        return join(
            state,
            jax.tree.map(
                lambda a, own: lax.dynamic_index_in_dim(a, source, 0, False).astype(own.dtype),
                gathered,
                x,
            ),
        )

    return lax.fori_loop(0, ahead, one, state)


def rms_scale(values):
    return lax.rsqrt(jnp.mean(values * values, axis=-1, keepdims=True) + norm_eps)


def norm_back(grad_unit, unit, scale):
    return scale * (grad_unit - unit * jnp.mean(grad_unit * unit, axis=-1, keepdims=True))


def silu_slope(values):
    sigma = jax.nn.sigmoid(values)
    return sigma * (1.0 + values * (1.0 - sigma))


def split_small(small):
    widths = [D, D, HEADS_M * HEAD_M, HEADS_M, HEADS_M, HEADS_M]
    pieces = []
    start = 0
    for count in widths:
        pieces.append(small[start : start + count])
        start += count
    return pieces


def span_terms(streams, writes, reads, raw_step, segment, before, step_bias, decay_log, skip):
    step_size = jax.nn.softplus(raw_step + step_bias)
    rates = -jnp.exp(decay_log) * step_size
    total = jnp.cumsum(rates, axis=0)
    length = segment.shape[0]
    order = jnp.arange(length)
    causal = (order[:, None] >= order[None, :]) & (segment[:, None] == segment[None, :])
    spread = total[:, None, :] - total[None, :, :]
    decays = jnp.exp(jnp.where(causal[:, :, None], spread, -1e30))
    intersections = jnp.dot(reads, writes.T, precision=highest, preferred_element_type=jnp.float32)
    scaled = streams * step_size[:, :, None]
    mixing = decays * intersections[:, :, None]
    local_out = (
        jnp.einsum("tsh,shp->thp", mixing, scaled, precision=highest)
        + skip[None, :, None] * streams
    )
    last = length - 1
    keep_last = segment == segment[last]
    to_end = jnp.exp(jnp.where(keep_last[:, None], total[last][None, :] - total, -1e30))
    state_part = jnp.einsum("sh,shp,sn->hpn", to_end, scaled, writes, precision=highest)
    entering = (segment == before).astype(jnp.float32)
    from_start = jnp.exp(total) * entering[:, None]
    through = from_start[last]
    return (local_out, state_part, through, from_start)


def chain(earlier, later):
    return (earlier[0] * later[0], later[0][:, :, None, None] * earlier[1] + later[1])


def adam_step(weight, grad, first, second, rate):
    first = beta_one * first + (1.0 - beta_one) * grad
    second = beta_two * second + (1.0 - beta_two) * grad * grad
    fixed_first = first / (1.0 - beta_one**STEP)
    fixed_second = second / (1.0 - beta_two**STEP)
    weight = weight - rate * (
        fixed_first / (jnp.sqrt(fixed_second) + adam_eps) + weight_decay * weight
    )
    return (weight, first, second)


def shards(
    block_input,
    segment_ids,
    cotangent,
    in_weight,
    out_weight,
    gate_up_weight,
    down_weight,
    in_first,
    out_first,
    gate_up_first,
    down_first,
    in_second,
    out_second,
    gate_up_second,
    down_second,
    small_params,
    small_first,
    small_second,
):
    batch, length, width = block_input.shape
    total_len = length * lax.axis_size("ctx")
    place = lax.axis_index("ctx")
    mixer_width = HEADS_M * HEAD_M
    query_width = QH * HD
    pair_width = KVH * HD
    group = QH // KVH
    scale = HD ** (-0.5)
    gain_in, gain_mid, gain_mix, step_bias, decay_log, skip = split_small(small_params)
    mixer_in, mixer_out = (
        lax.all_gather(in_weight.astype(jnp.bfloat16), ("dp", "ctx"), axis=0, tiled=True),
        lax.all_gather(out_weight.astype(jnp.bfloat16), ("dp", "ctx"), axis=0, tiled=True),
    )
    tokens = block_input.astype(jnp.float32)
    scale_in = rms_scale(tokens)
    unit_in = tokens * scale_in
    normed = (unit_in * gain_in).astype(jnp.bfloat16)
    project = jnp.einsum("std,df->stf", normed, mixer_in, preferred_element_type=jnp.float32)
    gate_z = project[..., :mixer_width]
    streams = project[..., mixer_width : 2 * mixer_width].reshape(batch, length, HEADS_M, HEAD_M)
    writes = project[..., 2 * mixer_width : 2 * mixer_width + STATE]
    reads = project[..., 2 * mixer_width + STATE : 2 * mixer_width + 2 * STATE]
    base = 2 * mixer_width + 2 * STATE + HEADS_M
    raw_step = project[..., 2 * mixer_width + 2 * STATE : base]
    queries = project[..., base : base + query_width].astype(jnp.bfloat16)
    keys = project[..., base + query_width : base + query_width + pair_width].astype(jnp.bfloat16)
    values = project[..., base + query_width + pair_width :].astype(jnp.bfloat16)
    all_keys, all_values, all_segs = (
        lax.all_gather(keys, "ctx", axis=1, tiled=True),
        lax.all_gather(values, "ctx", axis=1, tiled=True),
        lax.all_gather(segment_ids.astype(jnp.bfloat16), "ctx", axis=1, tiled=True),
    )
    all_segs = all_segs.astype(jnp.int32)
    prev_place = jnp.maximum(place * length - 1, 0)
    before = lax.dynamic_slice_in_dim(all_segs, prev_place, 1, 1)[:, 0]
    before = jnp.where(place > 0, before, -1)
    query_groups = queries.reshape(batch, length, KVH, group, HD)
    key_groups = all_keys.reshape(batch, total_len, KVH, HD)
    value_groups = all_values.reshape(batch, total_len, KVH, HD)
    query_place = place * length + jnp.arange(length)
    key_place = jnp.arange(total_len)
    allowed = (key_place[None, None, :] <= query_place[None, :, None]) & (
        all_segs[:, None, :] == segment_ids[:, :, None]
    )

    def raw_scores():
        scores = (
            jnp.einsum(
                "sqkgd,spkd->skgqp", query_groups, key_groups, preferred_element_type=jnp.float32
            )
            * scale
        )
        return jnp.where(allowed[:, None, None, :, :], scores, -1e30)

    scores = raw_scores()
    peak = jnp.max(scores, axis=-1, keepdims=True)
    log_total = peak + jnp.log(jnp.sum(jnp.exp(scores - peak), axis=-1, keepdims=True))
    shares_low = jnp.exp(scores - log_total).astype(jnp.bfloat16)
    attended = jnp.einsum(
        "skgqp,spkd->sqkgd", shares_low, value_groups, preferred_element_type=jnp.float32
    ).reshape(batch, length, query_width)
    local_map = jax.vmap(span_terms, in_axes=(0, 0, 0, 0, 0, 0, None, None, None))

    def local_part(
        part_streams, part_writes, part_reads, part_raw, part_bias, part_decay, part_skip
    ):
        return local_map(
            part_streams,
            part_writes,
            part_reads,
            part_raw,
            segment_ids,
            before,
            part_bias,
            part_decay,
            part_skip,
        )

    (local_out, state_part, through, from_start), ssd_back = jax.vjp(
        local_part, streams, writes, reads, raw_step, step_bias, decay_log, skip
    )
    identity = (jnp.ones_like(through), jnp.zeros_like(state_part))
    carried, state_in = prefix((through, state_part), "ctx", chain, identity)
    read_state = jnp.einsum("stn,shpn->sthp", reads, state_in, precision=highest)
    scanned = (local_out + from_start[..., None] * read_state).reshape(batch, length, mixer_width)
    gate_act = jax.nn.silu(gate_z)
    gated = scanned * gate_act
    scale_mix = rms_scale(gated)
    unit_mix = gated * scale_mix
    joined = jnp.concatenate([unit_mix * gain_mix, attended], axis=-1).astype(jnp.bfloat16)
    mixed = jnp.einsum("stf,fd->std", joined, mixer_out, preferred_element_type=jnp.float32)
    middle = tokens + mixed
    mlp_in, mlp_out = (
        lax.all_gather(gate_up_weight.astype(jnp.bfloat16), ("dp", "ctx"), axis=0, tiled=True),
        lax.all_gather(down_weight.astype(jnp.bfloat16), ("dp", "ctx"), axis=0, tiled=True),
    )
    scale_mid = rms_scale(middle)
    unit_mid = middle * scale_mid
    normed_mid = (unit_mid * gain_mid).astype(jnp.bfloat16)
    gate_up = jnp.einsum("std,df->stf", normed_mid, mlp_in, preferred_element_type=jnp.float32)
    gate = gate_up[..., :FF]
    upper = gate_up[..., FF:]
    hidden = (jax.nn.silu(gate) * upper).astype(jnp.bfloat16)
    result = middle + jnp.einsum("stf,fd->std", hidden, mlp_out, preferred_element_type=jnp.float32)
    block_output = result.astype(jnp.bfloat16)
    back = cotangent.astype(jnp.float32)
    mlp_in, mlp_out = (
        lax.all_gather(gate_up_weight.astype(jnp.bfloat16), ("dp", "ctx"), axis=0, tiled=True),
        lax.all_gather(down_weight.astype(jnp.bfloat16), ("dp", "ctx"), axis=0, tiled=True),
    )
    grad_down = jnp.einsum("stf,std->fd", hidden, cotangent, preferred_element_type=jnp.float32)
    grad_hidden = jnp.einsum("std,fd->stf", cotangent, mlp_out, preferred_element_type=jnp.float32)
    grad_gu = jnp.concatenate(
        [grad_hidden * upper * silu_slope(gate), grad_hidden * jax.nn.silu(gate)], axis=-1
    ).astype(jnp.bfloat16)
    grad_gate_up = jnp.einsum(
        "std,stf->df", normed_mid, grad_gu, preferred_element_type=jnp.float32
    )
    grad_normed_mid = jnp.einsum("stf,df->std", grad_gu, mlp_in, preferred_element_type=jnp.float32)
    grad_gain_mid = jnp.sum(grad_normed_mid * unit_mid, axis=(0, 1))
    grad_middle = back + norm_back(grad_normed_mid * gain_mid, unit_mid, scale_mid)
    mlp_grad_in, mlp_grad_out = (
        lax.psum_scatter(grad_gate_up, ("dp", "ctx"), scatter_dimension=0, tiled=True),
        lax.psum_scatter(grad_down, ("dp", "ctx"), scatter_dimension=0, tiled=True),
    )
    mixer_in, mixer_out = (
        lax.all_gather(in_weight.astype(jnp.bfloat16), ("dp", "ctx"), axis=0, tiled=True),
        lax.all_gather(out_weight.astype(jnp.bfloat16), ("dp", "ctx"), axis=0, tiled=True),
    )
    grad_mixed = grad_middle.astype(jnp.bfloat16)
    grad_out = jnp.einsum("stf,std->fd", joined, grad_mixed, preferred_element_type=jnp.float32)
    grad_joined = jnp.einsum(
        "std,fd->stf", grad_mixed, mixer_out, preferred_element_type=jnp.float32
    )
    grad_attended = grad_joined[..., mixer_width:].astype(jnp.bfloat16)
    scores = raw_scores()
    shares = jnp.exp(scores - log_total)
    grad_att = grad_attended.reshape(batch, length, KVH, group, HD)
    grad_shares = jnp.einsum(
        "sqkgd,spkd->skgqp", grad_att, value_groups, preferred_element_type=jnp.float32
    )
    inner = jnp.sum(grad_shares * shares, axis=-1, keepdims=True)
    grad_scores = (shares * (grad_shares - inner)).astype(jnp.bfloat16)
    grad_queries = (
        jnp.einsum("skgqp,spkd->sqkgd", grad_scores, key_groups, preferred_element_type=jnp.float32)
        * scale
    )
    grad_keys = (
        jnp.einsum(
            "skgqp,sqkgd->spkd", grad_scores, query_groups, preferred_element_type=jnp.float32
        )
        * scale
    )
    grad_values = jnp.einsum(
        "skgqp,sqkgd->spkd",
        shares.astype(jnp.bfloat16),
        grad_att,
        preferred_element_type=jnp.float32,
    )
    own_keys, own_values = (
        lax.psum_scatter(
            grad_keys.reshape(batch, total_len, pair_width).astype(jnp.bfloat16),
            "ctx",
            scatter_dimension=1,
            tiled=True,
        ).astype(jnp.float32),
        lax.psum_scatter(
            grad_values.reshape(batch, total_len, pair_width).astype(jnp.bfloat16),
            "ctx",
            scatter_dimension=1,
            tiled=True,
        ).astype(jnp.float32),
    )
    grad_mix_part = grad_joined[..., :mixer_width]
    grad_gain_mix = jnp.sum(grad_mix_part * unit_mix, axis=(0, 1))
    grad_gated = norm_back(grad_mix_part * gain_mix, unit_mix, scale_mix)
    grad_scan = (grad_gated * gate_act).reshape(batch, length, HEADS_M, HEAD_M)
    grad_z = grad_gated * scanned * silu_slope(gate_z)
    grad_from = jnp.sum(grad_scan * read_state, axis=-1)
    grad_read = grad_scan * from_start[..., None]
    grad_state_in = jnp.einsum("sthp,stn->shpn", grad_read, reads, precision=highest)
    grad_reads_extra = jnp.einsum("sthp,shpn->stn", grad_read, state_in, precision=highest)
    carried_back, grad_state_out = carried_in((through, grad_state_in), "ctx", chain, identity)
    grad_through = jnp.sum(grad_state_out * state_in, axis=(2, 3))
    grad_streams, grad_writes, grad_reads, grad_raw, grad_bias, grad_decay, grad_skip = ssd_back(
        (grad_scan, grad_state_out, grad_through, grad_from)
    )
    grad_reads = grad_reads + grad_reads_extra
    grad_project = jnp.concatenate(
        [
            grad_z,
            grad_streams.reshape(batch, length, mixer_width),
            grad_writes,
            grad_reads,
            grad_raw,
            grad_queries.reshape(batch, length, query_width),
            own_keys,
            own_values,
        ],
        axis=-1,
    ).astype(jnp.bfloat16)
    grad_in = jnp.einsum("std,stf->df", normed, grad_project, preferred_element_type=jnp.float32)
    grad_normed = jnp.einsum(
        "stf,df->std", grad_project, mixer_in, preferred_element_type=jnp.float32
    )
    grad_gain_in = jnp.sum(grad_normed * unit_in, axis=(0, 1))
    input_grad = grad_middle + norm_back(grad_normed * gain_in, unit_in, scale_in)
    mixer_grad_in, mixer_grad_out = (
        lax.psum_scatter(grad_in, ("dp", "ctx"), scatter_dimension=0, tiled=True),
        lax.psum_scatter(grad_out, ("dp", "ctx"), scatter_dimension=0, tiled=True),
    )
    small_grad = lax.psum(
        jnp.concatenate(
            [grad_gain_in, grad_gain_mid, grad_gain_mix, grad_bias, grad_decay, grad_skip]
        ),
        ("dp", "ctx"),
    )
    new_in = adam_step(in_weight, mixer_grad_in, in_first, in_second, rate_scale / math.sqrt(D))
    new_out = adam_step(
        out_weight,
        mixer_grad_out,
        out_first,
        out_second,
        rate_scale / math.sqrt(HEADS_M * HEAD_M + QH * HD),
    )
    new_gate_up = adam_step(
        gate_up_weight, mlp_grad_in, gate_up_first, gate_up_second, rate_scale / math.sqrt(D)
    )
    new_down = adam_step(
        down_weight, mlp_grad_out, down_first, down_second, rate_scale / math.sqrt(FF)
    )
    new_small = adam_step(small_params, small_grad, small_first, small_second, small_rate)
    return (
        block_output,
        input_grad,
        new_in[0],
        new_in[1],
        new_in[2],
        new_out[0],
        new_out[1],
        new_out[2],
        new_gate_up[0],
        new_gate_up[1],
        new_gate_up[2],
        new_down[0],
        new_down[1],
        new_down[2],
        new_small[0],
        new_small[1],
        new_small[2],
    )


def solution(mesh):
    return jax.shard_map(
        shards,
        mesh=mesh,
        in_specs=(
            P("dp", "ctx", None),
            P("dp", "ctx"),
            P("dp", "ctx", None),
            P(("dp", "ctx"), None),
            P(("dp", "ctx"), None),
            P(("dp", "ctx"), None),
            P(("dp", "ctx"), None),
            P(("dp", "ctx"), None),
            P(("dp", "ctx"), None),
            P(("dp", "ctx"), None),
            P(("dp", "ctx"), None),
            P(("dp", "ctx"), None),
            P(("dp", "ctx"), None),
            P(("dp", "ctx"), None),
            P(("dp", "ctx"), None),
            P(),
            P(),
            P(),
        ),
        out_specs=(
            P("dp", "ctx", None),
            P("dp", "ctx", None),
            P(("dp", "ctx"), None),
            P(("dp", "ctx"), None),
            P(("dp", "ctx"), None),
            P(("dp", "ctx"), None),
            P(("dp", "ctx"), None),
            P(("dp", "ctx"), None),
            P(("dp", "ctx"), None),
            P(("dp", "ctx"), None),
            P(("dp", "ctx"), None),
            P(("dp", "ctx"), None),
            P(("dp", "ctx"), None),
            P(("dp", "ctx"), None),
            P(),
            P(),
            P(),
        ),
        check_vma=False,
    )
```

profile of v0, /device:TPU:0, one launch (start us, length us, event | category | flops | bytes accessed | tf_op | source)
XLA Modules:
  0.0 3128.9 jit_solution(617223825064284162)
XLA Ops:
  12.3 199.3 %all-gather.11.cloned.1.call-done = bf16[2048,8240]{1,0:T(8,128)(2,1)} async-done(((bf16[64,8240]{1,0:T(8,128)(2,1)}), bf16[2048,8240]{1,0:T(8,128)(2,1)}) %all-gather.11.cloned.1.call-update) | async-done | bytes 33751056 | tf_op jit(solution)/shard_map/all_gather | solution.py:167
  211.6 26.7 fusion.194
  289.2 15.5 fusion.22
  304.6 14.5 exponential_reduce_fusion
  319.2 16.1 convolution_convert_fusion.1
  335.4 12.2 while.29
  354.7 68.0 %fusion.29 = f32[1,512,48,64]{1,3,2,0:T(8,128)S(1)} fusion(f32[512,48,64]{0,2,1:T(8,128)S(1)} %fusion.72, f32[1,512,48,64]{1,3,2,0:T(8,128)} %bitcast.470, f32[512,48]{0,1:T(8,128)S(1)} %bitcast.511, f32[48]{0:T(128)S(1)} %copy-done.72, f32[512,512]{1,0:T(8,128)S(1)} %copy-done.34, f32[512,48]{0,1:T(8,128)S(1)} %copy-done.48, ...), kind=kOutput, calls=%fused_computation.52 | convolution fusion | flops 9709289472 | bytes 26771648 | tf_op jit(solution)/shard_map/jvp(vmap(tsh,shp->thp))/dot_general | solution.py:109
  440.7 14.7 multiply_reduce_fusion.6
  455.5 181.5 %all-gather.19.cloned.1.call-done = bf16[2048,8192]{1,0:T(8,128)(2,1)} async-done(((bf16[64,8192]{1,0:T(8,128)(2,1)}), bf16[2048,8192]{1,0:T(8,128)(2,1)}) %all-gather.19.cloned.1.call-update) | async-done | bytes 33554448 | tf_op jit(solution)/shard_map/all_gather | solution.py:250
  637.0 28.1 convolution_bitcast_fusion.1
  665.1 88.4 %all-gather.21.cloned.1.call-done = bf16[4096,2048]{1,0:T(8,128)(2,1)} async-done(((bf16[128,2048]{1,0:T(8,128)(2,1)}), bf16[4096,2048]{1,0:T(8,128)(2,1)}) %all-gather.21.cloned.1.call-update) | async-done | bytes 16777232 | tf_op jit(solution)/shard_map/all_gather | solution.py:251
  753.5 22.0 fusion.65
  775.6 26.8 fusion.59
  807.1 16.4 convolution_bitcast_fusion.2
  828.3 11.3 multiply_reduce_fusion
  854.1 24.8 fusion.6
  878.9 28.8 fusion.24
  907.7 12.2 fusion.83
  920.0 17.0 fusion.84
  937.1 18.3 fusion.82
  957.0 18.0 fusion.91
  975.7 31.6 %fusion.43 = f32[2048,8192]{1,0:T(8,128)} fusion(bf16[512,4096]{1,0:T(8,128)(2,1)} %get-tuple-element.309, bf16[512,4096]{1,0:T(8,128)(2,1)} %get-tuple-element.308, f32[1,512,2048]{2,1,0:T(8,128)} %get-tuple-element.330, f32[2048]{0:T(1024)S(1)} %copy-done.39, f32[512]{0:T(512)S(1)} %copy-done.41), kind=kOutput, calls=%fused_computation.85 | convolution fusion | flops 17199792128 | bytes 79702016 | tf_op jit(solution)/shard_map/std,stf->df/dot_general | solution.py:272
  1008.6 65.4 %fusion.10 = (f32[512,48]{0,1:T(8,128)}, f32[512,48]{0,1:T(8,128)}, f32[512,512]{1,0:T(8,128)S(1)}) fusion(f32[512,512]{1,0:T(8,128)S(1)} %copy-done.35, f32[512,48]{0,1:T(8,128)S(1)} %copy-done.49, pred[512,512]{1,0:T(8,128)(4,1)} %fusion.134, f32[48,64,512]{2,1,0:T(8,128)} %bitcast.483, f32[512,48,64]{0,2,1:T(8,128)} %bitcast.471, ...), kind=kOutput, calls=%fused_computation.23 | convolution fusion | flops 9778184192 | bytes 15335424 | tf_op jit(solution)/shard_map/transpose(jvp(vmap(tsh,shp->thp)))/dot_general | solution.py:109
  1110.9 9.5 fusion.31
  1130.9 45.0 %multiply_reduce_fusion.3 = (f32[512,48]{0,1:T(8,128)S(1)}, bf16[1,512,48,64]{1,3,2,0:T(8,128)(2,1)S(1)}) fusion(f32[1,512,48,64]{1,3,2,0:T(8,128)} %bitcast.473, f32[512,48]{0,1:T(8,128)S(1)} %copy-done.31, f32[1,512,48,64]{1,3,2,0:T(8,128)} %bitcast.484, f32[48]{0:T(128)} %get-tuple-element.320, f32[48,64,512]{2,1,0:T(8,128)} %bitcast.485, ...), kind=kOutput, calls=%fused_computation.65 | convolution fusion | flops 9713983488 | bytes 30015680 | tf_op jit(solution)/shard_map/transpose(jvp(vmap(tsh,shp->thp)))/dot_general | solution.py:109
  1193.7 32.7 %fusion.135 = f32[2048,8240]{1,0:T(8,128)} fusion(bf16[512,8240]{0,1:T(8,128)(2,1)} %bitcast_dynamic-update-slice_fusion.1, bf16[1,512,2048]{2,1,0:T(8,128)(2,1)} %param.22, f32[2048]{0:T(1024)S(1)} %copy-done.55, f32[512]{0:T(512)S(1)} %copy-done.66), kind=kOutput, calls=%fused_computation.182 | convolution fusion | flops 17284726784 | bytes 78047232 | tf_op jit(solution)/shard_map/std,stf->df/dot_general | solution.py:358
  1227.3 15.5 fusion.63
  1242.9 26.4 fusion.55
  1269.5 44.6 %psum.7 = f32[7312]{0:T(1024)S(1)} all-reduce(f32[7312]{0:T(1024)S(1)} %concatenate.63), channel_id=1, replica_groups=mesh['dp'=8,'ctx'=4] {'dp','ctx'}, use_global_device_ids=true, to_apply=%region_37.38 | all-reduce | flops 7312 | bytes 58496 | tf_op jit(solution)/shard_map/psum | solution.py:368
  1332.3 356.0 %reduce-scatter.17.cloned.1.call-done = f32[128,2048]{1,0:T(8,128)} async-done(((f32[4096,2048]{1,0:T(8,128)}), f32[128,2048]{1,0:T(8,128)}) %reduce-scatter.17.cloned.1.call-update) | async-done | bytes 1048592 | tf_op jit(solution)/shard_map/reduce_scatter | solution.py:280
  1692.1 704.5 %reduce-scatter.15.cloned.1.call-done = f32[64,8192]{1,0:T(8,128)} async-done(((f32[2048,8192]{1,0:T(8,128)}), f32[64,8192]{1,0:T(8,128)}) %reduce-scatter.15.cloned.1.call-update) | async-done | bytes 2097168 | tf_op jit(solution)/shard_map/reduce_scatter | solution.py:279
  2403.8 711.6 %reduce-scatter.11.cloned.1.call-done = f32[64,8240]{1,0:T(8,128)} async-done(((f32[2048,8240]{1,0:T(8,128)}), f32[64,8240]{1,0:T(8,128)}) %reduce-scatter.11.cloned.1.call-update) | async-done | bytes 2109456 | tf_op jit(solution)/shard_map/reduce_scatter | solution.py:365
  (321 shorter events, 229.5 us)
Async XLA Ops:
  7.2 204.4 %copy-start.14 = (bf16[1,512,2048]{2,1,0:T(8,128)(2,1)S(1)}, bf16[1,512,2048]{2,1,0:T(8,128)(2,1)}, u32[]{:S(2)}) copy-start(bf16[1,512,2048]{2,1,0:T(8,128)(2,1)} %param.22) | copy-start | bytes 6291460
  7.2 204.4 %all-gather.11.cloned.1.call-start = ((), (), s32[]{:S(2)}) async-start(), calls=%async_computation.6 | async-start | bytes 35143680 | tf_op jit(solution)/shard_map/all_gather | solution.py:167
  10.1 279.1 %all-gather.15.cloned.1.call-start = ((), (), s32[]{:S(2)}) async-start(), calls=%async_computation.8 | async-start | bytes 1310720 | tf_op jit(solution)/shard_map/all_gather | solution.py:185
  12.3 226.0 %copy-start.65 = (f32[512]{0:T(512)}, f32[512]{0:T(512)S(1)}, u32[]{:S(2)}) copy-start(f32[512]{0:T(512)S(1)} %add_rsqrt_fusion.2) | copy-start | bytes 6148
  12.3 226.0 %copy-start.54 = (f32[2048]{0:T(1024)}, f32[2048]{0:T(1024)S(1)}, u32[]{:S(2)}) copy-start(f32[2048]{0:T(1024)S(1)} %get-tuple-element.319) | copy-start | bytes 24580
  12.3 790.1 %copy-start.38 = (f32[2048]{0:T(1024)}, f32[2048]{0:T(1024)S(1)}, u32[]{:S(2)}) copy-start(f32[2048]{0:T(1024)S(1)} %get-tuple-element.318) | copy-start | bytes 24580
  240.1 79.1 %all-gather.13.cloned.1.call-start = ((), (), s32[]{:S(2)}) async-start(), calls=%async_computation.7 | async-start | bytes 1310720 | tf_op jit(solution)/shard_map/all_gather | solution.py:186
  254.6 80.8 %all-gather.23.cloned.1.call-start = ((), (), s32[]{:S(2)}) async-start(), calls=%async_computation.18 | async-start | bytes 7864320 | tf_op jit(solution)/shard_map/all_gather | solution.py:32
  255.8 98.9 %copy-start.30 = (f32[512,48]{0,1:T(8,128)}, f32[512,48]{0,1:T(8,128)S(1)}, u32[]{:S(2)}) copy-start(f32[512,48]{0,1:T(8,128)S(1)} %get-tuple-element.311) | copy-start | bytes 294916
  267.2 173.6 %all-gather.17.cloned.1.call-start = ((), (), s32[]{:S(2)}) async-start(), calls=%async_computation.9 | async-start | bytes 17301504 | tf_op jit(solution)/shard_map/all_gather | solution.py:168
  268.1 368.9 %all-gather.19.cloned.1.call-start = ((), (), s32[]{:S(2)}) async-start(), calls=%async_computation.10 | async-start | bytes 34603008 | tf_op jit(solution)/shard_map/all_gather | solution.py:250
  269.3 484.2 %all-gather.21.cloned.1.call-start = ((), (), s32[]{:S(2)}) async-start(), calls=%async_computation.11 | async-start | bytes 17301504 | tf_op jit(solution)/shard_map/all_gather | solution.py:251
  271.4 827.7 %all-gather.25.cloned.1.call-start = ((), (), s32[]{:S(2)}) async-start(), calls=%async_computation.19 | async-start | bytes 7864320 | tf_op jit(solution)/shard_map/all_gather | solution.py:53
  347.6 75.1 %copy-start = (f32[1,48,64,256]{3,2,1,0:T(8,128)}, f32[1,48,64,256]{3,2,1,0:T(8,128)S(1)}, u32[]{:S(2)}) copy-start(f32[1,48,64,256]{3,2,1,0:T(8,128)S(1)} %get-tuple-element.195) | copy-start | bytes 9437188
  347.6 75.1 %copy-start.71 = (bf16[4,1,48]{2,1,0:T(2,128)(2,1)}, bf16[4,1,48]{2,1,0:T(2,128)(2,1)S(1)}, u32[]{:S(2)}) copy-start(bf16[4,1,48]{2,1,0:T(2,128)(2,1)S(1)} %get-tuple-element.499) | copy-start | bytes 1156
  455.5 346.9 %copy-start.40 = (f32[512]{0:T(512)}, f32[512]{0:T(512)S(1)}, u32[]{:S(2)}) copy-start(f32[512]{0:T(512)S(1)} %add_rsqrt_fusion) | copy-start | bytes 6148
  637.0 116.5 %copy-start.26 = (bf16[1,512,2048]{2,1,0:T(8,128)(2,1)S(1)}, bf16[1,512,2048]{2,1,0:T(8,128)(2,1)}, u32[]{:S(2)}) copy-start(bf16[1,512,2048]{2,1,0:T(8,128)(2,1)} %param.24) | copy-start | bytes 6291460
  852.3 338.0 %reduce-scatter.7.cloned.1.call-start = ((), (), s32[]{:S(2)}) async-start(), calls=%async_computation.12 | async-start | bytes 1310720 | tf_op jit(solution)/shard_map/reduce_scatter | solution.py:317
  919.9 272.1 %reduce-scatter.9.cloned.1.call-start = ((), (), s32[]{:S(2)}) async-start(), calls=%async_computation.13 | async-start | bytes 1310720 | tf_op jit(solution)/shard_map/reduce_scatter | solution.py:323
  937.0 391.2 %reduce-scatter.13.cloned.1.call-start = ((), (), s32[]{:S(2)}) async-start(), calls=%async_computation.15 | async-start | bytes 34603008 | tf_op jit(solution)/shard_map/reduce_scatter | solution.py:366
  955.5 732.9 %reduce-scatter.17.cloned.1.call-start = ((), (), s32[]{:S(2)}) async-start(), calls=%async_computation.17 | async-start | bytes 34603008 | tf_op jit(solution)/shard_map/reduce_scatter | solution.py:280
  975.0 1421.6 %reduce-scatter.15.cloned.1.call-start = ((), (), s32[]{:S(2)}) async-start(), calls=%async_computation.16 | async-start | bytes 69206016 | tf_op jit(solution)/shard_map/reduce_scatter | solution.py:279
  1007.3 71.3 %slice-start.4 = ((s8[6291456]{0:T(1024)(128)(4,1)}), s8[2097152]{0:T(1024)(128)(4,1)S(1)}, s32[]{:S(2)}) async-start(s8[6291456]{0:T(1024)(128)(4,1)} %bitcast.480), calls=%async_computation.24 | async-start | bytes 4194304
  1007.3 2108.0 %reduce-scatter.11.cloned.1.call-start = ((), (), s32[]{:S(2)}) async-start(), calls=%async_computation.14 | async-start | bytes 70287360 | tf_op jit(solution)/shard_map/reduce_scatter | solution.py:365
  1007.4 78.2 %slice-start.8 = ((s8[6291456]{0:T(1024)(128)(4,1)}), s8[4194304]{0:T(1024)(128)(4,1)S(1)}, s32[]{:S(2)}) async-start(s8[6291456]{0:T(1024)(128)(4,1)} %bitcast.489), calls=%async_computation.28 | async-start | bytes 8388608
  1008.5 70.0 %slice-start.5 = ((s8[6291456]{0:T(1024)(128)(4,1)}), s8[4194304]{0:T(1024)(128)(4,1)S(1)}, s32[]{:S(2)}) async-start(s8[6291456]{0:T(1024)(128)(4,1)} %bitcast.480), calls=%async_computation.25 | async-start | bytes 8388608
  1008.5 77.0 %slice-start.9 = ((s8[6291456]{0:T(1024)(128)(4,1)}), s8[2097152]{0:T(1024)(128)(4,1)S(1)}, s32[]{:S(2)}) async-start(s8[6291456]{0:T(1024)(128)(4,1)} %bitcast.489), calls=%async_computation.29 | async-start | bytes 4194304
  1242.9 71.2 %copy-start.56 = (f32[7312]{0:T(1024)S(1)}, f32[7312]{0:T(1024)}, u32[]{:S(2)}) copy-start(f32[7312]{0:T(1024)} %param.38) | copy-start | bytes 87748
  1242.9 71.2 %copy-start.57 = (f32[7312]{0:T(1024)S(1)}, f32[7312]{0:T(1024)}, u32[]{:S(2)}) copy-start(f32[7312]{0:T(1024)} %param.39) | copy-start | bytes 87748
  1321.4 367.0 %copy-start.19 = (f32[128,2048]{1,0:T(8,128)S(1)}, f32[128,2048]{1,0:T(8,128)}, u32[]{:S(2)}) copy-start(f32[128,2048]{1,0:T(8,128)} %param.28) | copy-start | bytes 3145732
  1321.4 367.0 %copy-start.33 = (f32[128,2048]{1,0:T(8,128)S(1)}, f32[128,2048]{1,0:T(8,128)}, u32[]{:S(2)}) copy-start(f32[128,2048]{1,0:T(8,128)} %param.32) | copy-start | bytes 3145732
  1692.1 1423.2 %copy-start.12 = (f32[64,8240]{1,0:T(8,128)S(1)}, f32[64,8240]{1,0:T(8,128)}, u32[]{:S(2)}) copy-start(f32[64,8240]{1,0:T(8,128)} %param.25) | copy-start | bytes 6328324
  (69 other events, 957.9 us)
Sparse Core Ops, SparseCore 0:
  11.5 200.0 all-gather.10
  240.3 14.8 all-gather.14
  257.3 16.7 all-gather.12
  276.1 46.4 all-gather.22
  325.8 114.8 all-gather.16
  444.0 192.9 all-gather.18
  640.4 113.0 all-gather.20
  852.5 44.5 all-gather.24
  920.0 22.7 reduce-scatter.6
  945.9 24.8 reduce-scatter.8
  973.1 355.0 reduce-scatter.12
  1330.4 357.9 reduce-scatter.16
  1690.7 705.8 reduce-scatter.14
  2398.8 716.4 reduce-scatter.10
where the time goes:
time: 3140 us; the launch traced here: 3130 us
  waiting for transfers between devices  2250 us (72%)
  matrix products  606 us (19%)
  other arithmetic  154 us (5%)
  blocking collectives  54.8 us (2%)
  local copies, waits for them, and re-layouts  43.3 us (1%)
    reduce_scatter x1, waiting for transfers between devices, shards(): lax.psum_scatter(grad_in, ('dp', 'ctx'), scatter_dimension=0, tiled=True)  712 us
    reduce_scatter x1, waiting for transfers between devices, shards(): lax.psum_scatter(grad_gate_up, ('dp', 'ctx'), scatter_dimension=0, tiled=...  704 us
    reduce_scatter x1, waiting for transfers between devices, shards(): lax.psum_scatter(grad_down, ('dp', 'ctx'), scatter_dimension=0, tiled=True)  356 us
    all_gather x1, waiting for transfers between devices, shards(): lax.all_gather(in_weight.astype(jnp.bfloat16), ('dp', 'ctx'), axis=0, til...  199 us
    all_gather x1, waiting for transfers between devices, shards(): lax.all_gather(gate_up_weight.astype(jnp.bfloat16), ('dp', 'ctx'), axis=0...  182 us
    dot_general x3, matrix products, span_terms(): jnp.einsum('tsh,shp->thp', mixing, scaled, precision=highest)  178 us
    all_gather x1, waiting for transfers between devices, shards(): lax.all_gather(down_weight.astype(jnp.bfloat16), ('dp', 'ctx'), axis=0, t...  88.4 us
  transfers between devices with their start and end apart: 14, of which 8 were waited for; matrix products, arithmetic and copies ran while one was open for 21% of the time, Pallas kernels for 0%

commit v1 on v0

v1 whole, which is shorter than its diff:
```python
import functools
import math

import jax
import jax.numpy as jnp
from jax import lax
from jax.experimental import pallas as pl
from jax.experimental.pallas import tpu as pltpu
from jax.sharding import PartitionSpec as P

D = 2048
FF = 4096
QH = 8
KVH = 2
HD = 128
HEADS_M = 48
HEAD_M = 64
STATE = 256
STEP = 10
DOC_MOST = 800
DSSM = HEADS_M * HEAD_M
SHARED = 2 * STATE + 2 * KVH * HD + 128
CHUNK = 256
QBLOCK = 256

norm_eps = 1e-05
beta_one = 0.9
beta_two = 0.95
adam_eps = 1e-08
weight_decay = 0.1
rate_scale = 3.0
small_rate = 0.3
bf16 = jnp.bfloat16
f32 = jnp.float32
NN = (((1,), (0,)), ((), ()))
NT = (((1,), (1,)), ((), ()))
TN = (((0,), (0,)), ((), ()))


def dot(a, b, dims=NN):
    return lax.dot_general(a, b, dims, preferred_element_type=f32)


def from_ctx(x, m):
    count = lax.axis_size("ctx")
    return lax.ppermute(x, "ctx", [(i ^ m, i) for i in range(count)])


def from_dp(x, j, k):
    count = lax.axis_size("dp")
    inner = count // 4
    pairs = []
    for i in range(count):
        z, w = divmod(i, inner)
        pairs.append((((z + j) % 4) * inner + (w + k) % inner, i))
    return lax.ppermute(x, "dp", pairs)


def to_dp(x, j, k):
    return from_dp(x, -j, -k)


ORDER = (2, 1, 3, 0)


def gather_dp(own):
    inner = lax.axis_size("dp") // 4
    blocks = {(0, 0): own}
    for j in (2, 1, 3):
        blocks[j, 0] = from_dp(own, j, 0)
    for j in (0, 1, 3, 2):
        for k in range(1, inner):
            blocks[j, k] = from_dp(blocks[j, 0], 0, k)
    return blocks


def dp_index(j, k):
    count = lax.axis_size("dp")
    inner = count // 4
    place = lax.axis_index("dp")
    return lax.rem(place // inner + j, 4) * inner + lax.rem(lax.rem(place, inner) + k, inner)


def place_dp(blocks):
    own = blocks[0, 0]
    full = jnp.zeros((lax.axis_size("dp"),) + own.shape, own.dtype)
    for (j, k), block in blocks.items():
        full = lax.dynamic_update_index_in_dim(full, block, dp_index(j, k), 0)
    return full


def scatter_dp(full):
    inner = lax.axis_size("dp") // 4

    def part(j, k):
        return lax.dynamic_index_in_dim(full, dp_index(j, k), 0, False)

    rows = {}
    for j in ORDER:
        total = part(j, 0).astype(f32)
        for k in range(1, inner):
            total = total + to_dp(part(j, k), 0, k).astype(f32)
        rows[j] = total
    total = rows[0]
    for j in (2, 1, 3):
        total = total + to_dp(rows[j].astype(bf16), j, 0).astype(f32)
    return total


def gather_ctx(own):
    count = lax.axis_size("ctx")
    blocks = {0: own}
    for m in range(2, count, 2):
        blocks[m] = from_ctx(own, m)
    for m in range(0, count, 2):
        blocks[m + 1] = from_ctx(blocks[m], 1)
    return blocks


def place_ctx(blocks):
    own = blocks[0]
    place = lax.axis_index("ctx")
    full = jnp.zeros((lax.axis_size("ctx"),) + own.shape, own.dtype)
    for m, block in blocks.items():
        full = lax.dynamic_update_index_in_dim(full, block, place ^ m, 0)
    return full


def scatter_ctx(part):
    count = lax.axis_size("ctx")
    sums = {}
    for m in [m for m in range(2, count, 2)] + [0]:
        sums[m] = part(m).astype(f32) + from_ctx(part(m + 1), 1).astype(f32)
    total = sums[0]
    for m in range(2, count, 2):
        total = total + from_ctx(sums[m].astype(bf16), m).astype(f32)
    return total


def exchange_ctx(blocks):
    place = lax.axis_index("ctx")
    got = {}
    for m in range(lax.axis_size("ctx")):
        own = lax.dynamic_index_in_dim(blocks, place ^ m, 0, False)
        got[m] = from_ctx(own, m) if m else own
    return place_ctx(got)


def sum_ctx(x):
    m = 1
    while m < lax.axis_size("ctx"):
        x = x + from_ctx(x, m)
        m *= 2
    return x


def split_cols(a, block):
    count = lax.axis_size("ctx")
    rows, n = a.shape
    a = a.reshape(rows, n // (count * block), count, block)
    return a.transpose(2, 0, 1, 3).reshape(count, rows, n // count)


def join_cols(a, block):
    count, rows, n = a.shape
    a = a.reshape(count, rows, n // block, block)
    return a.transpose(1, 2, 0, 3).reshape(rows, count * n)


def own_cols(a, block):
    count = lax.axis_size("ctx")
    rows, n = a.shape
    a = a.reshape(rows, n // (count * block), count, block)
    a = lax.dynamic_index_in_dim(a, lax.axis_index("ctx"), 2, False)
    return a.reshape(rows, n // count)


def spread_cols(a, block):
    count = lax.axis_size("ctx")
    rows, n = a.shape
    a = a.reshape(rows, n // block, block)
    full = jnp.zeros((rows, n // block, count, block), a.dtype)
    full = lax.dynamic_update_index_in_dim(full, a, lax.axis_index("ctx"), 2)
    return full.reshape(rows, count * n)


def attention_window(total_len):
    reach = -(-(DOC_MOST - 1) // QBLOCK) * QBLOCK
    return min(reach, total_len - QBLOCK), min(reach + QBLOCK, total_len)


def attention_scores(total_len, q_ref, k_ref, col_ref, row_ref):
    back, window = attention_window(total_len)
    first = pl.program_id(1) * QBLOCK
    start = pl.multiple_of(jnp.maximum(first - back, 0), QBLOCK)
    keys = k_ref[pl.ds(start, window), :]
    scores = dot(q_ref[...], keys, NT) * HD ** (-0.5)
    query_place = first + lax.broadcasted_iota(jnp.int32, (QBLOCK, window), 0)
    key_place = start + lax.broadcasted_iota(jnp.int32, (QBLOCK, window), 1)
    key_seg = row_ref[0:1, pl.ds(start, window)]
    allowed = (key_place <= query_place) & (col_ref[:, 0:1] == key_seg)
    return start, window, keys, jnp.where(allowed, scores, -1e30)


def attend_kernel(total_len, q_ref, k_ref, v_ref, col_ref, row_ref, out_ref, log_ref):
    start, window, _, scores = attention_scores(total_len, q_ref, k_ref, col_ref, row_ref)
    peak = jnp.max(scores, axis=1, keepdims=True)
    expo = jnp.exp(scores - peak)
    log_total = peak + jnp.log(jnp.sum(expo, axis=1, keepdims=True))
    shares = jnp.exp(scores - log_total).astype(bf16)
    out_ref[...] = dot(shares, v_ref[pl.ds(start, window), :]).astype(out_ref.dtype)
    log_ref[...] = jnp.broadcast_to(log_total, log_ref.shape)


def attend_back_kernel(
    total_len, q_ref, k_ref, v_ref, col_ref, row_ref, log_ref, grad_ref, dq_ref, dk_ref, dv_ref
):
    @pl.when(pl.program_id(1) == 0)
    def _():
        dk_ref[...] = jnp.zeros_like(dk_ref)
        dv_ref[...] = jnp.zeros_like(dv_ref)

    start, window, keys, scores = attention_scores(total_len, q_ref, k_ref, col_ref, row_ref)
    shares = jnp.exp(scores - log_ref[:, 0:1])
    grad = grad_ref[...]
    grad_shares = dot(grad, v_ref[pl.ds(start, window), :], NT)
    inner = jnp.sum(shares * grad_shares, axis=1, keepdims=True)
    grad_scores = (shares * (grad_shares - inner)).astype(bf16)
    scale = HD ** (-0.5)
    dq_ref[...] = dot(grad_scores, keys) * scale
    span = pl.ds(start, window)
    dk_ref[span, :] += dot(grad_scores, q_ref[...], TN) * scale
    dv_ref[span, :] += dot(shares.astype(bf16), grad, TN)


def attention_specs(total_len):
    tile = pl.BlockSpec((QBLOCK, HD), lambda h, i: (i, h))
    whole = pl.BlockSpec((total_len, HD), lambda h, i: (0, h))
    col = pl.BlockSpec((QBLOCK, 128), lambda h, i: (i, 0))
    row = pl.BlockSpec((8, total_len), lambda h, i: (0, 0))
    return tile, whole, col, row


def attention_call(queries, keys, values, seg_col, seg_row):
    total_len, width = queries.shape
    tile, whole, col, row = attention_specs(total_len)
    return pl.pallas_call(
        functools.partial(attend_kernel, total_len),
        grid=(width // HD, total_len // QBLOCK),
        in_specs=[tile, whole, whole, col, row],
        out_specs=[tile, tile],
        out_shape=[
            jax.ShapeDtypeStruct((total_len, width), bf16),
            jax.ShapeDtypeStruct((total_len, width), f32),
        ],
        compiler_params=pltpu.CompilerParams(vmem_limit_bytes=48 * 2**20),
        cost_estimate=pl.CostEstimate(
            flops=4 * total_len * 1280 * width, bytes_accessed=12 * total_len * width, transcendentals=0
        ),
        name="attend",
    )(queries, keys, values, seg_col, seg_row)


def attention_back_call(queries, keys, values, seg_col, seg_row, log_total, grad):
    total_len, width = queries.shape
    tile, whole, col, row = attention_specs(total_len)
    return pl.pallas_call(
        functools.partial(attend_back_kernel, total_len),
        grid=(width // HD, total_len // QBLOCK),
        in_specs=[tile, whole, whole, col, row, tile, tile],
        out_specs=[tile, whole, whole],
        out_shape=[jax.ShapeDtypeStruct((total_len, width), f32)] * 3,
        compiler_params=pltpu.CompilerParams(vmem_limit_bytes=48 * 2**20),
        cost_estimate=pl.CostEstimate(
            flops=10 * total_len * 1280 * width, bytes_accessed=24 * total_len * width, transcendentals=0
        ),
        name="attend_back",
    )(queries, keys, values, seg_col, seg_row, log_total, grad)


def pair_of(col, offset, j, left):
    a = offset + 2 * j
    return jnp.where(left, col[:, a : a + 1], col[:, a + 1 : a + 2])


def state_decay(col, j, left_rows):
    last = col[CHUNK - 1 : CHUNK, :]
    a = 64 + 2 * j
    return jnp.where(left_rows, last[:, a : a + 1], last[:, a + 1 : a + 2])


def scan_kernel(pairs, x_ref, k_ref, r_ref, col_ref, row_ref, skip_ref, y_ref, s_ref, state):
    @pl.when(pl.program_id(0) == 0)
    def _():
        state[...] = jnp.zeros_like(state)

    writes = k_ref[...].astype(bf16)
    reads = r_ref[...].astype(bf16)
    col = col_ref[...]
    row = row_ref[...]
    entering = state[...].astype(bf16)
    s_ref[0] = entering
    products = dot(reads, writes, NT)
    later = lax.broadcasted_iota(jnp.int32, (CHUNK, CHUNK), 0)
    earlier = lax.broadcasted_iota(jnp.int32, (CHUNK, CHUNK), 1)
    mask = (later >= earlier) & (col[:, 127:128] == row[16:17, :])
    left = lax.broadcasted_iota(jnp.int32, (CHUNK, 128), 1) < HEAD_M
    left_rows = lax.broadcasted_iota(jnp.int32, (128, STATE), 0) < HEAD_M
    through = dot(reads, entering, NT)
    for j in range(pairs):
        lanes = slice(128 * j, 128 * j + 128)
        x = x_ref[:, lanes]
        scaled = x * pair_of(col, 32, j, left)
        scaled_low = scaled.astype(bf16)
        outs = []
        for h in (2 * j, 2 * j + 1):
            spread = col[:, h : h + 1] - row[h : h + 1, :]
            mixing = jnp.exp(jnp.where(mask, spread, -1e30)) * products
            outs.append(dot(mixing.astype(bf16), scaled_low))
        y_ref[:, lanes] = (
            jnp.where(left, outs[0], outs[1])
            + pair_of(col, 64, j, left) * through[:, lanes]
            + skip_ref[0:1, lanes] * x
        )
        to_end = (scaled * pair_of(col, 96, j, left)).astype(bf16)
        state[lanes, :] = state_decay(col, j, left_rows) * state[lanes, :] + dot(to_end, writes, TN)


def scan_back_kernel(
    pairs,
    x_ref,
    k_ref,
    r_ref,
    col_ref,
    row_ref,
    skip_ref,
    y_ref,
    s_ref,
    dy_ref,
    sum_ref,
    dx_ref,
    dk_ref,
    dr_ref,
    red_ref,
    tot_ref,
    adjoint,
    keep,
):
    @pl.when(pl.program_id(0) == 0)
    def _():
        adjoint[...] = jnp.zeros_like(adjoint)

    writes = k_ref[...].astype(bf16)
    reads = r_ref[...].astype(bf16)
    col = col_ref[...]
    row = row_ref[...]
    entering = s_ref[0]
    products = dot(writes, reads, NT)
    earlier = lax.broadcasted_iota(jnp.int32, (CHUNK, CHUNK), 0)
    later = lax.broadcasted_iota(jnp.int32, (CHUNK, CHUNK), 1)
    mask = (later >= earlier) & (col[:, 127:128] == row[16:17, :])
    left = lax.broadcasted_iota(jnp.int32, (CHUNK, 128), 1) < HEAD_M
    left_rows = lax.broadcasted_iota(jnp.int32, (128, STATE), 0) < HEAD_M
    incoming = adjoint[...]
    incoming_low = incoming.astype(bf16)
    values = dot(writes, incoming_low, NT)
    grad_products = jnp.zeros((CHUNK, CHUNK), f32)
    grad_writes = jnp.zeros((CHUNK, STATE), f32)
    grad_reads = jnp.zeros((CHUNK, STATE), f32)
    tot_ref[0] = jnp.zeros(tot_ref.shape[1:], f32)
    for j in range(pairs):
        lanes = slice(128 * j, 128 * j + 128)
        x = x_ref[:, lanes]
        step = pair_of(col, 32, j, left)
        scaled = x * step
        scaled_low = scaled.astype(bf16)
        dy = dy_ref[:, lanes]
        dy_low = dy.astype(bf16)
        grads = []
        for side, h in enumerate((2 * j, 2 * j + 1)):
            spread = row[h : h + 1, :] - col[:, h : h + 1]
            decay = jnp.exp(jnp.where(mask, spread, -1e30))
            half = left if side == 0 else jnp.logical_not(left)
            grad_mixing = dot(jnp.where(half, scaled_low, jnp.zeros_like(scaled_low)), dy_low, NT)
            grad_products += grad_mixing * decay
            grads.append(dot((decay * products).astype(bf16), dy_low))
        grad_scaled = jnp.where(left, grads[0], grads[1])
        decay_end = pair_of(col, 96, j, left)
        to_end = (scaled * decay_end).astype(bf16)
        passed = to_end.astype(f32) * values[:, lanes]
        skip = skip_ref[0:1, lanes]
        flow = (
            dy_low.astype(f32) * (y_ref[:, lanes] - skip * x)
            - scaled_low.astype(f32) * grad_scaled
            - passed
        )
        grad_scaled += decay_end * values[:, lanes]
        dx_ref[:, lanes] = step * grad_scaled + skip * dy
        from_start = (pair_of(col, 64, j, left) * dy).astype(bf16)
        grad_reads += dot(from_start, entering[lanes, :])
        grad_writes += dot(to_end, incoming_low[lanes, :])
        pieces = (flow, x * grad_scaled)
        for n, piece in enumerate(pieces):
            high = piece.astype(bf16)
            keep[2 * n, :, lanes] = high
            keep[2 * n + 1, :, lanes] = (piece - high.astype(f32)).astype(bf16)
        tot_ref[0, 1:2, lanes] = jnp.sum(passed, axis=0, keepdims=True)
        tot_ref[0, 2:3, lanes] = jnp.sum(dy * x, axis=0, keepdims=True)
        product = incoming[lanes, :] * entering[lanes, :].astype(f32)
        high = product.astype(bf16)
        low = (product - high.astype(f32)).astype(bf16)
        ones = jnp.ones((8, STATE), bf16)
        tot_ref[0, 0:1, lanes] = (dot(ones, high, NT) + dot(ones, low, NT))[0:1, :]
        adjoint[lanes, :] = state_decay(col, j, left_rows) * incoming[lanes, :] + dot(
            from_start, reads, TN
        )
    grad_products = grad_products.astype(bf16)
    dk_ref[...] = grad_writes + dot(grad_products, reads)
    dr_ref[...] = grad_reads + dot(grad_products, writes, TN)
    sums = sum_ref[...]
    red_ref[...] = (
        dot(keep[0], sums[0]) + dot(keep[1], sums[0]) + dot(keep[2], sums[1]) + dot(keep[3], sums[1])
    )


def scan_call(own, shared, col, row, skip, width):
    total_len = own.shape[0]
    count = total_len // CHUNK
    return pl.pallas_call(
        functools.partial(scan_kernel, width // 128),
        grid=(count,),
        in_specs=[
            pl.BlockSpec((CHUNK, width), lambda i: (i, 1)),
            pl.BlockSpec((CHUNK, STATE), lambda i: (i, 0)),
            pl.BlockSpec((CHUNK, STATE), lambda i: (i, 1)),
            pl.BlockSpec((CHUNK, 128), lambda i: (i, 0)),
            pl.BlockSpec((24, CHUNK), lambda i: (0, i)),
            pl.BlockSpec((8, width), lambda i: (0, 0)),
        ],
        out_specs=[
            pl.BlockSpec((CHUNK, width), lambda i: (i, 0)),
            pl.BlockSpec((1, width, STATE), lambda i: (i, 0, 0)),
        ],
        out_shape=[
            jax.ShapeDtypeStruct((total_len, width), f32),
            jax.ShapeDtypeStruct((count, width, STATE), bf16),
        ],
        scratch_shapes=[pltpu.VMEM((width, STATE), f32)],
        compiler_params=pltpu.CompilerParams(vmem_limit_bytes=48 * 2**20),
        cost_estimate=pl.CostEstimate(
            flops=8 * total_len * width * STATE, bytes_accessed=12 * total_len * width, transcendentals=0
        ),
        name="state_scan",
    )(own, shared, shared, col, row, skip)


def scan_back_call(own, shared, col, row, skip, scanned, states, grad, width):
    total_len = own.shape[0]
    count = total_len // CHUNK
    owner = jnp.arange(width)[:, None] // HEAD_M
    lane = jnp.arange(128)[None, :]
    sums = jnp.stack([owner == lane, owner + 32 == lane]).astype(bf16)

    def back(i):
        return count - 1 - i

    return pl.pallas_call(
        functools.partial(scan_back_kernel, width // 128),
        grid=(count,),
        in_specs=[
            pl.BlockSpec((CHUNK, width), lambda i: (back(i), 1)),
            pl.BlockSpec((CHUNK, STATE), lambda i: (back(i), 0)),
            pl.BlockSpec((CHUNK, STATE), lambda i: (back(i), 1)),
            pl.BlockSpec((CHUNK, 128), lambda i: (back(i), 0)),
            pl.BlockSpec((24, CHUNK), lambda i: (0, back(i))),
            pl.BlockSpec((8, width), lambda i: (0, 0)),
            pl.BlockSpec((CHUNK, width), lambda i: (back(i), 0)),
            pl.BlockSpec((1, width, STATE), lambda i: (back(i), 0, 0)),
            pl.BlockSpec((CHUNK, width), lambda i: (back(i), 0)),
            pl.BlockSpec((2, width, 128), lambda i: (0, 0, 0)),
        ],
        out_specs=[
            pl.BlockSpec((CHUNK, width), lambda i: (back(i), 0)),
            pl.BlockSpec((CHUNK, STATE), lambda i: (back(i), 0)),
            pl.BlockSpec((CHUNK, STATE), lambda i: (back(i), 0)),
            pl.BlockSpec((CHUNK, 128), lambda i: (back(i), 0)),
            pl.BlockSpec((1, 8, width), lambda i: (back(i), 0, 0)),
        ],
        out_shape=[
            jax.ShapeDtypeStruct((total_len, width), f32),
            jax.ShapeDtypeStruct((total_len, STATE), f32),
            jax.ShapeDtypeStruct((total_len, STATE), f32),
            jax.ShapeDtypeStruct((total_len, 128), f32),
            jax.ShapeDtypeStruct((count, 8, width), f32),
        ],
        scratch_shapes=[pltpu.VMEM((width, STATE), f32), pltpu.VMEM((4, CHUNK, width), bf16)],
        compiler_params=pltpu.CompilerParams(vmem_limit_bytes=48 * 2**20),
        cost_estimate=pl.CostEstimate(
            flops=20 * total_len * width * STATE, bytes_accessed=24 * total_len * width, transcendentals=0
        ),
        name="state_scan_back",
    )(own, shared, shared, col, row, skip, scanned, states, grad, sums)


def rms_scale(values):
    return lax.rsqrt(jnp.mean(values * values, axis=-1, keepdims=True) + norm_eps)


def norm_back(grad_unit, unit, scale):
    return scale * (grad_unit - unit * jnp.mean(grad_unit * unit, axis=-1, keepdims=True))


def silu_slope(values):
    sigma = jax.nn.sigmoid(values)
    return sigma * (1.0 + values * (1.0 - sigma))


def split_small(small):
    widths = [D, D, DSSM, HEADS_M, HEADS_M, HEADS_M]
    pieces = []
    start = 0
    for count in widths:
        pieces.append(small[start : start + count])
        start += count
    return pieces


def adam_step(weight, grad, first, second, rate):
    first = beta_one * first + (1.0 - beta_one) * grad
    second = beta_two * second + (1.0 - beta_two) * grad * grad
    fixed_first = first / (1.0 - beta_one**STEP)
    fixed_second = second / (1.0 - beta_two**STEP)
    weight = weight - rate * (
        fixed_first / (jnp.sqrt(fixed_second) + adam_eps) + weight_decay * weight
    )
    return (weight, first, second)


def pad_lanes(a, width):
    return jnp.pad(a, ((0, 0), (0, width - a.shape[1])))


def shards(
    block_input,
    segment_ids,
    cotangent,
    in_weight,
    out_weight,
    gate_up_weight,
    down_weight,
    in_first,
    out_first,
    gate_up_first,
    down_first,
    in_second,
    out_second,
    gate_up_second,
    down_second,
    small_params,
    small_first,
    small_second,
):
    peers = lax.axis_size("ctx")
    groups = lax.axis_size("dp")
    place = lax.axis_index("ctx")
    length = block_input.shape[0] * block_input.shape[1]
    total_len = length * peers
    row_block = out_weight.shape[0]
    in_rows = in_weight.shape[0]
    strided = row_block == HD
    width = DSSM // peers
    heads = HEADS_M // peers
    query_heads = QH // peers
    query_width = query_heads * HD
    own_width = 2 * width + query_width
    ff_width = FF // peers
    pair_block = 2 * HEAD_M if strided else width
    query_block = HD if strided else query_width
    head_block = 2 if strided else heads
    gain_in, gain_mid, gain_mix, step_bias, decay_log, skip = split_small(small_params)

    x_own = block_input.reshape(length, D)
    x_blocks = gather_ctx(x_own)
    segments = place_ctx(gather_ctx(segment_ids.reshape(length))).reshape(total_len)

    in_low = in_weight.astype(bf16)
    base = 2 * DSSM + 2 * STATE + HEADS_M
    query_end = base + QH * HD
    shared_low = jnp.concatenate(
        [
            in_low[:, 2 * DSSM : 2 * DSSM + 2 * STATE],
            in_low[:, query_end:],
            in_low[:, 2 * DSSM + 2 * STATE : base],
            jnp.zeros((in_rows, 128 - HEADS_M), bf16),
        ],
        axis=1,
    )
    own_low = jnp.concatenate(
        [
            split_cols(in_low[:, :DSSM], pair_block),
            split_cols(in_low[:, DSSM : 2 * DSSM], pair_block),
            split_cols(in_low[:, base:query_end], query_block),
        ],
        axis=2,
    )
    own_rows = exchange_ctx(own_low).reshape(peers * in_rows, own_width)
    w_own = place_dp(gather_dp(own_rows)).reshape(D, own_width)
    shared_rows = place_dp(gather_dp(shared_low))
    w_shared = place_ctx(gather_ctx(shared_rows))
    w_shared = w_shared.transpose(1, 0, 2, 3).reshape(D, SHARED)
    out_low = out_weight.astype(bf16)
    if strided:
        w_out = place_dp(gather_dp(out_low)).reshape(width + query_width, D)
    else:
        whole_out = lax.all_gather(out_low, ("dp", "ctx"), axis=0, tiled=True)
        w_out = jnp.concatenate(
            [
                lax.dynamic_slice_in_dim(whole_out, place * width, width, 0),
                lax.dynamic_slice_in_dim(whole_out, DSSM + place * query_width, query_width, 0),
            ],
            axis=0,
        )
    gu_low = gate_up_weight.astype(bf16)
    gu_low = jnp.concatenate(
        [split_cols(gu_low[:, :FF], row_block), split_cols(gu_low[:, FF:], row_block)], axis=2
    )
    w_gate_up = exchange_ctx(gu_low).reshape(peers * in_rows, 2 * ff_width)
    w_gate_up = place_dp(gather_dp(w_gate_up)).reshape(D, 2 * ff_width)
    w_down = place_dp(gather_dp(down_weight.astype(bf16))).reshape(ff_width, D)
    cot_blocks = gather_ctx(cotangent.reshape(length, D))

    tokens = place_ctx(x_blocks).reshape(total_len, D).astype(f32)
    scale_in = rms_scale(tokens)
    unit_in = tokens * scale_in
    normed = (unit_in * gain_in).astype(bf16)
    shared = dot(normed, w_shared)
    own = dot(normed, w_own)
    gate_z = own[:, :width]
    queries = own[:, 2 * width :].astype(bf16)
    keys = shared[:, 2 * STATE : 2 * STATE + KVH * HD].astype(bf16)
    values = shared[:, 2 * STATE + KVH * HD : 2 * STATE + 2 * KVH * HD].astype(bf16)
    raw_step = own_cols(shared[:, SHARED - 128 : SHARED - 128 + HEADS_M], head_block)
    if query_heads < KVH:
        own_kv = (place * query_heads * KVH // QH) * HD
        keys = lax.dynamic_slice_in_dim(keys, own_kv, query_width, 1)
        values = lax.dynamic_slice_in_dim(values, own_kv, query_width, 1)
    own_bias = own_cols(step_bias[None, :], head_block)
    own_decay = jnp.exp(own_cols(decay_log[None, :], head_block))
    own_skip = jnp.repeat(own_cols(skip[None, :], head_block), HEAD_M, axis=1)
    own_skip = jnp.broadcast_to(own_skip, (8, width))
    own_gain_mix = own_cols(gain_mix[None, :], pair_block)

    chunks = total_len // CHUNK
    step = jax.nn.softplus(raw_step + own_bias)
    rates = (-own_decay * step).reshape(chunks, CHUNK, heads)
    order = jnp.arange(CHUNK)
    lower = (order[:, None] >= order[None, :]).astype(f32)
    running = jnp.einsum("ts,csh->cth", lower, rates, precision=lax.Precision.HIGHEST)
    seg_chunks = segments.reshape(chunks, CHUNK)
    seg_last = seg_chunks[:, -1:]
    seg_before = jnp.concatenate([jnp.full((1, 1), -1, seg_last.dtype), seg_last[:-1]], axis=0)
    from_start = jnp.exp(running) * (seg_chunks == seg_before).astype(f32)[:, :, None]
    to_end = jnp.exp(
        jnp.where((seg_chunks == seg_last)[:, :, None], running[:, -1:, :] - running, -1e30)
    )
    seg_float = segments.astype(f32)
    running = running.reshape(total_len, heads)
    col = jnp.concatenate(
        [
            pad_lanes(running, 32),
            pad_lanes(step, 32),
            pad_lanes(from_start.reshape(total_len, heads), 32),
            pad_lanes(to_end.reshape(total_len, heads), 31),
            seg_float[:, None],
        ],
        axis=1,
    )
    row = jnp.concatenate(
        [
            jnp.pad(running.T, ((0, 16 - heads), (0, 0))),
            jnp.broadcast_to(seg_float[None, :], (8, total_len)),
        ],
        axis=0,
    )
    seg_col = jnp.broadcast_to(seg_float[:, None], (total_len, 128))
    seg_row = jnp.broadcast_to(seg_float[None, :], (8, total_len))

    scanned, states = scan_call(own, shared, col, row, own_skip, width)
    attended, log_total = attention_call(queries, keys, values, seg_col, seg_row)
    gate_act = jax.nn.silu(gate_z)
    gated = scanned * gate_act
    square = sum_ctx(jnp.sum(gated * gated, axis=-1))
    scale_mix = lax.rsqrt(square / DSSM + norm_eps)[:, None]
    unit_mix = gated * scale_mix
    joined = jnp.concatenate([(unit_mix * own_gain_mix).astype(bf16), attended], axis=1)
    mixed_part = dot(joined, w_out).astype(bf16).reshape(peers, length, D)
    mixed = scatter_ctx(lambda m: lax.dynamic_index_in_dim(mixed_part, place ^ m, 0, False))

    middle = x_own.astype(f32) + mixed
    scale_mid = rms_scale(middle)
    unit_mid = middle * scale_mid
    mid_blocks = gather_ctx((unit_mid * gain_mid).astype(bf16))
    normed_mid = jnp.concatenate([mid_blocks[m] for m in range(peers)], axis=0)
    cot = jnp.concatenate([cot_blocks[m] for m in range(peers)], axis=0)
    gate_up = dot(normed_mid, w_gate_up)
    gate = gate_up[:, :ff_width]
    upper = gate_up[:, ff_width:]
    hidden = (jax.nn.silu(gate) * upper).astype(bf16)
    result_part = dot(hidden, w_down).astype(bf16).reshape(peers, length, D)
    result = middle + scatter_ctx(lambda m: result_part[m])
    block_output = result.astype(bf16).reshape(block_input.shape)
    grad_down = dot(hidden, cot, TN).astype(bf16)
    grad_hidden = dot(cot, w_down, NT)
    grad_gu = jnp.concatenate(
        [grad_hidden * upper * silu_slope(gate), grad_hidden * jax.nn.silu(gate)], axis=1
    ).astype(bf16)
    grad_gate_up = dot(normed_mid, grad_gu, TN).astype(bf16)
    back_part = dot(grad_gu, w_gate_up, NT).astype(bf16).reshape(peers, length, D)
    grad_normed_mid = scatter_ctx(lambda m: back_part[m])
    grad_gain_mid = jnp.sum(grad_normed_mid * unit_mid, axis=0)
    grad_middle = cotangent.reshape(length, D).astype(f32) + norm_back(
        grad_normed_mid * gain_mid, unit_mid, scale_mid
    )
    grad_mixed = place_ctx(gather_ctx(grad_middle.astype(bf16))).reshape(total_len, D)
    sum_down = scatter_dp(grad_down.reshape(groups, row_block, D))
    sum_gate_up = scatter_dp(grad_gate_up.reshape(groups, peers * in_rows, 2 * ff_width))

    grad_out = dot(joined, grad_mixed, TN)
    if strided:
        sum_out = scatter_dp(grad_out.astype(bf16).reshape(groups, row_block, D))
    else:
        spread = jnp.zeros((DSSM + QH * HD, D), f32)
        spread = lax.dynamic_update_slice_in_dim(spread, grad_out[:width], place * width, 0)
        spread = lax.dynamic_update_slice_in_dim(
            spread, grad_out[width:], DSSM + place * query_width, 0
        )
        sum_out = lax.psum_scatter(spread, ("dp", "ctx"), scatter_dimension=0, tiled=True)
    grad_joined = dot(grad_mixed, w_out, NT)
    grad_attended = grad_joined[:, width:].astype(bf16)
    grad_mix_part = grad_joined[:, :width]
    grad_unit = grad_mix_part * own_gain_mix
    inner = sum_ctx(jnp.sum(grad_unit * unit_mix, axis=-1))[:, None] / DSSM
    grad_queries, grad_keys, grad_values = attention_back_call(
        queries, keys, values, seg_col, seg_row, log_total, grad_attended
    )
    grad_gain_mix = jnp.sum(grad_mix_part * unit_mix, axis=0)
    grad_gated = scale_mix * (grad_unit - unit_mix * inner)
    grad_scan = grad_gated * gate_act
    grad_z = grad_gated * scanned * silu_slope(gate_z)
    grad_streams, grad_writes, grad_reads, reduced, totals = scan_back_call(
        own, shared, col, row, own_skip, scanned, states, grad_scan, width
    )
    totals = totals.reshape(chunks, 8, heads, HEAD_M).sum(axis=3)
    last = from_start[:, -1, :] * totals[:, 0, :] + totals[:, 1, :]
    flow = reduced[:, :heads].reshape(chunks, CHUNK, heads)
    grad_rate = jnp.einsum("ts,cth->csh", lower, flow, precision=lax.Precision.HIGHEST)
    grad_rate = (grad_rate + last[:, None, :]).reshape(total_len, heads)
    grad_step = reduced[:, 32 : 32 + heads] - own_decay * grad_rate
    grad_raw = grad_step * jax.nn.sigmoid(raw_step + own_bias)
    grad_bias = jnp.sum(grad_raw, axis=0)
    grad_decay = jnp.sum(grad_rate * rates.reshape(total_len, heads), axis=0)
    grad_skip = jnp.sum(totals[:, 2, :], axis=0)
    if query_heads < KVH:
        blank = jnp.zeros((total_len, KVH * HD), f32)
        grad_keys = lax.dynamic_update_slice_in_dim(blank, grad_keys, own_kv, 1)
        grad_values = lax.dynamic_update_slice_in_dim(blank, grad_values, own_kv, 1)
    grad_own = jnp.concatenate(
        [grad_z.astype(bf16), grad_streams.astype(bf16), grad_queries.astype(bf16)], axis=1
    )
    grad_shared = jnp.concatenate(
        [
            grad_writes.astype(bf16),
            grad_reads.astype(bf16),
            grad_keys.astype(bf16),
            grad_values.astype(bf16),
            pad_lanes(spread_cols(grad_raw.astype(bf16), head_block), 128),
        ],
        axis=1,
    )
    grad_in_own = dot(normed, grad_own, TN).astype(bf16)
    grad_in_shared = dot(normed, grad_shared, TN).astype(bf16)
    sum_own = scatter_dp(grad_in_own.reshape(groups, peers * in_rows, own_width))
    shared_part = grad_in_shared.reshape(groups, peers, in_rows, SHARED)
    sum_shared = scatter_ctx(
        lambda m: lax.dynamic_index_in_dim(shared_part, place ^ m, 1, False)
    ).astype(bf16)
    sum_shared = scatter_dp(sum_shared)
    normed_part = (dot(grad_own, w_own, NT) + dot(grad_shared, w_shared, NT)).astype(bf16)
    normed_part = normed_part.reshape(peers, length, D)
    grad_normed = scatter_ctx(lambda m: lax.dynamic_index_in_dim(normed_part, place ^ m, 0, False))
    x_float = x_own.astype(f32)
    own_scale = rms_scale(x_float)
    own_unit = x_float * own_scale
    grad_gain_in = jnp.sum(grad_normed * own_unit, axis=0)
    input_grad = grad_middle + norm_back(grad_normed * gain_in, own_unit, own_scale)
    input_grad = input_grad.reshape(block_input.shape)

    got = exchange_ctx(sum_own.astype(bf16).reshape(peers, in_rows, own_width)).astype(f32)
    sum_in = jnp.concatenate(
        [
            join_cols(got[:, :, :width], pair_block),
            join_cols(got[:, :, width : 2 * width], pair_block),
            sum_shared[:, : 2 * STATE],
            sum_shared[:, SHARED - 128 : SHARED - 128 + HEADS_M],
            join_cols(got[:, :, 2 * width :], query_block),
            sum_shared[:, 2 * STATE : SHARED - 128],
        ],
        axis=1,
    )
    got = exchange_ctx(sum_gate_up.astype(bf16).reshape(peers, in_rows, 2 * ff_width)).astype(f32)
    sum_gate_up = jnp.concatenate(
        [join_cols(got[:, :, :ff_width], row_block), join_cols(got[:, :, ff_width:], row_block)],
        axis=1,
    )
    small_grad = lax.psum(
        jnp.concatenate(
            [
                grad_gain_in,
                grad_gain_mid,
                spread_cols(grad_gain_mix[None, :], pair_block)[0],
                spread_cols(grad_bias[None, :], head_block)[0],
                spread_cols(grad_decay[None, :], head_block)[0],
                spread_cols(grad_skip[None, :], head_block)[0],
            ]
        ),
        ("dp", "ctx"),
    )
    new_in = adam_step(in_weight, sum_in, in_first, in_second, rate_scale / math.sqrt(D))
    new_out = adam_step(
        out_weight, sum_out, out_first, out_second, rate_scale / math.sqrt(DSSM + QH * HD)
    )
    new_gate_up = adam_step(
        gate_up_weight, sum_gate_up, gate_up_first, gate_up_second, rate_scale / math.sqrt(D)
    )
    new_down = adam_step(
        down_weight, sum_down, down_first, down_second, rate_scale / math.sqrt(FF)
    )
    new_small = adam_step(small_params, small_grad, small_first, small_second, small_rate)
    return (block_output, input_grad) + new_in + new_out + new_gate_up + new_down + new_small


def solution(mesh):
    rows = P(("dp", "ctx"), None)
    tokens = P("dp", "ctx", None)
    return jax.shard_map(
        shards,
        mesh=mesh,
        in_specs=(tokens, P("dp", "ctx"), tokens) + (rows,) * 12 + (P(),) * 3,
        out_specs=(tokens, tokens) + (rows,) * 12 + (P(),) * 3,
        check_vma=False,
    )
```

time: 3140 us -> 1680 us (0.54)
  waiting for transfers between devices: 2250 us -> 800 us
  matrix products: 606 us -> 269 us
  starting transfers between devices: 0.84 us -> 142 us
  local copies, waits for them, and re-layouts: 43.3 us -> 174 us
  Pallas kernels: 0 us -> 105 us
    reduce_scatter x6 -> x0, waiting for transfers between devices: 1780 us -> none  [the longest x1 712 us: shards(): lax.psum_scatter(grad_in, ('dp', 'ctx'), scatter_dimension=0, tiled=True)]
    ppermute x0 -> x119, waiting for transfers between devices: none -> 800 us  [the longest x70 453 us: from_dp(): return lax.ppermute(x, 'dp', pairs)]
    all_gather x8 -> x0, waiting for transfers between devices: 475 us -> none  [the longest x1 199 us: shards(): lax.all_gather(in_weight.astype(jnp.bfloat16), ('dp', 'ctx'), axis=0, til...]
    dot_general x30 -> x17, matrix products: 606 us -> 269 us  [the longest x15 267 us: dot(): return lax.dot_general(a, b, dims, preferred_element_type=f32)]
    ppermute x0 -> x119, starting transfers between devices: none -> 142 us  [the longest x70 116 us: from_dp(): return lax.ppermute(x, 'dp', pairs)]
    pallas_call x0 -> x4, Pallas kernels: none -> 105 us  [the longest x1 33.3 us: scan_back_call(): pl.pallas_call(functools.partial(scan_back_kernel, width // 128), grid=(c...]
    convert_element_type x13 -> x23, other arithmetic: 8.82 us -> 64.4 us  [the longest x2 17.4 us: shards(): normed = (unit_in * gain_in).astype(bf16)]
    dynamic_update_slice x0 -> x70, local copies, waits for them, and re-layouts: none -> 45.1 us  [the longest x38 24.6 us: place_dp(): full = lax.dynamic_update_index_in_dim(full, block, dp_index(j, k), 0)]
  transfers between devices with their start and end apart: 14 -> 119, of which waited for: 8 -> 51; matrix products, arithmetic and copies ran while one was open for 21% -> 29% of each run, Pallas kernels for 0% -> 6%
where the time goes in v1:
time: 1680 us; the launch traced here: 1670 us
  waiting for transfers between devices  800 us (48%)
  matrix products  269 us (16%)
  local copies, waits for them, and re-layouts  174 us (10%)
  starting transfers between devices  142 us (8%)
  other arithmetic  138 us (8%)
  Pallas kernels  105 us (6%)
  blocking collectives  37 us (2%)
    ppermute x70, waiting for transfers between devices, from_dp(): return lax.ppermute(x, 'dp', pairs)  453 us
    ppermute x49, waiting for transfers between devices, from_ctx(): return lax.ppermute(x, 'ctx', [(i ^ m, i) for i in range(count)])  347 us
    dot_general x15, matrix products, dot(): return lax.dot_general(a, b, dims, preferred_element_type=f32)  267 us
    ppermute x70, starting transfers between devices, from_dp(): return lax.ppermute(x, 'dp', pairs)  116 us
    psum x1, blocking collectives, shards(): lax.psum(jnp.concatenate([grad_gain_in, grad_gain_mid, spread_cols(grad_g...  37 us
    unnamed x270, local copies, waits for them, and re-layouts  34.9 us
  transfers between devices with their start and end apart: 119, of which 51 were waited for; matrix products, arithmetic and copies ran while one was open for 29% of the time, Pallas kernels for 6%

profile of v1, /device:TPU:0, one launch (start us, length us, event | category | flops | bytes accessed | tf_op | source)
XLA Modules:
  0.0 1669.8 jit_solution(12702453864764492424)
XLA Ops:
  57.3 39.1 %collective-permute-done.4 = bf16[64,1792]{1,0:T(8,128)(2,1)S(1)} collective-permute-done((bf16[64,1792]{1,0:T(8,128)(2,1)}, bf16[64,1792]{1,0:T(8,128)(2,1)S(1)}, u32[]{:S(2)}, u32[]{:S(2)}) %collective-permute-start.4) | collective-permute-done | bytes 229408 | tf_op jit(solution)/shard_map/ppermute | solution.py:46
  179.2 30.8 %collective-permute-done.7 = bf16[256,1792]{1,0:T(8,128)(2,1)S(1)} collective-permute-done((bf16[256,1792]{1,0:T(8,128)(2,1)}, bf16[256,1792]{1,0:T(8,128)(2,1)S(1)}, u32[]{:S(2)}, u32[]{:S(2)}) %collective-permute-start.7) | collective-permute-done | bytes 917536 | tf_op jit(solution)/shard_map/ppermute | solution.py:56
  213.4 25.7 %collective-permute-done.20 = bf16[8,64,1152]{2,1,0:T(8,128)(2,1)S(1)} collective-permute-done((bf16[8,64,1152]{2,1,0:T(8,128)(2,1)S(1)}, bf16[8,64,1152]{2,1,0:T(8,128)(2,1)S(1)}, u32[]{:S(2)}, u32[]{:S(2)}) %collective-permute-start.20) | collective-permute-done | bytes 1179680 | tf_op jit(solution)/shard_map/ppermute | solution.py:46
  243.5 19.0 %collective-permute-done.10 = bf16[256,1792]{1,0:T(8,128)(2,1)S(1)} collective-permute-done((bf16[256,1792]{1,0:T(8,128)(2,1)S(1)}, bf16[256,1792]{1,0:T(8,128)(2,1)S(1)}, u32[]{:S(2)}, u32[]{:S(2)}) %collective-permute-start.10) | collective-permute-done | bytes 917536 | tf_op jit(solution)/shard_map/ppermute | solution.py:56
  263.0 19.1 %collective-permute-done.11 = bf16[256,1792]{1,0:T(8,128)(2,1)S(1)} collective-permute-done((bf16[256,1792]{1,0:T(8,128)(2,1)S(1)}, bf16[256,1792]{1,0:T(8,128)(2,1)S(1)}, u32[]{:S(2)}, u32[]{:S(2)}) %collective-permute-start.11) | collective-permute-done | bytes 917536 | tf_op jit(solution)/shard_map/ppermute | solution.py:56
  355.2 21.4 %fusion.115.x_ref = f32[2048,1792]{1,0:T(8,128)} fusion(bf16[2048,2048]{1,0:T(8,128)(2,1)} %bitcast.500, bf16[2048,1792]{1,0:T(8,128)(2,1)} %bitcast.511), kind=kOutput, calls=%fused_computation.356 | convolution fusion | flops 15032385536 | bytes 30408704 | tf_op jit(solution)/shard_map/dot_general | solution.py:41
  383.0 24.6 %state_scan.1 = (f32[2048,768]{1,0:T(8,128)}, bf16[8,768,256]{2,1,0:T(8,128)(2,1)S(1)}) custom-call(f32[2048,1792]{1,0:T(8,128)} %fusion.115.x_ref, f32[2048,1152]{1,0:T(8,128)} %copy.197.k_ref.r_ref, f32[2048,1152]{1,0:T(8,128)} %copy.197.k_ref.r_ref, f32[2048,128]{1,0:T(8,128)S(1)} %copy.199.col_ref, f32[24,2048]{1,0:T(8,128)S(1)} %select_maximum_fusion.row_ref, ...), custom_call_target="tpu_custom_call" | custom-call | flops 3221225472 | bytes 18874368 | tf_op jit(solution)/shard_map/state_scan/pallas_call | solution.py:429
  422.2 19.0 %attend.1 = (bf16[2048,256]{1,0:T(8,128)(2,1)S(1)}, f32[2048,256]{1,0:T(8,128)}) custom-call(bf16[2048,256]{1,0:T(8,128)(2,1)S(1)} %slice.294.q_ref, bf16[2048,256]{1,0:T(8,128)(2,1)S(1)} %get-tuple-element.105.k_ref, bf16[2048,256]{1,0:T(8,128)(2,1)S(1)} %get-tuple-element.104.v_ref, f32[2048,128]{1,0:T(8,128)S(1)} %broadcast_in_dim.352.col_ref, ...), custom_call_target="tpu_custom_call" | custom-call | flops 2684354560 | bytes 6291456 | tf_op jit(solution)/shard_map/attend/pallas_call | solution.py:247
  499.0 25.6 %collective-permute-done.37 = bf16[512,2048]{1,0:T(8,128)(2,1)S(1)} collective-permute-done((bf16[512,2048]{1,0:T(8,128)(2,1)S(1)}, bf16[512,2048]{1,0:T(8,128)(2,1)S(1)}, u32[]{:S(2)}, u32[]{:S(2)}) %collective-permute-start.37) | collective-permute-done | bytes 2097184 | tf_op jit(solution)/shard_map/ppermute | solution.py:46
  600.8 29.0 %collective-permute-done.62 = bf16[512,2048]{1,0:T(8,128)(2,1)} collective-permute-done((bf16[512,2048]{1,0:T(8,128)(2,1)S(1)}, bf16[512,2048]{1,0:T(8,128)(2,1)}, u32[]{:S(2)}, u32[]{:S(2)}) %collective-permute-start.62) | collective-permute-done | bytes 2097184 | tf_op jit(solution)/shard_map/ppermute | solution.py:46
  645.2 27.2 %fusion.39 = f32[2048,2048]{0,1:T(8,128)} fusion(bf16[2048,2048]{1,0:T(8,128)(2,1)} %bitcast.83, bf16[512,2048]{1,0:T(8,128)(2,1)} %copy-done.113, bf16[512,2048]{1,0:T(8,128)(2,1)} %copy-done.111, bf16[512,2048]{1,0:T(8,128)(2,1)} %copy-done.112, bf16[512,2048]{1,0:T(8,128)(2,1)} %copy-done.52), kind=kOutput, calls=%fused_computation.115 | convolution fusion | flops 17213423616 | bytes 33554432 | tf_op jit(solution)/shard_map/dot_general | solution.py:41
  672.4 19.0 %multiply_convert_fusion.2 = (bf16[2048,1024]{0,1:T(8,128)(2,1)}, bf16[2048,1024]{0,1:T(8,128)(2,1)}, bf16[2048,1024]{0,1:T(8,128)(2,1)S(1)}) fusion(f32[2048,2048]{0,1:T(8,128)} %fusion.39, bf16[1024,2048]{1,0:T(8,128)(2,1)} %bitcast.92, bf16[512,2048]{1,0:T(8,128)(2,1)} %collective-permute-done.63, bf16[512,2048]{1,0:T(8,128)(2,1)} %collective-permute-done.62, ...), kind=kOutput, calls=%fused_computation.10 | convolution fusion | flops 8654946304 | bytes 41943040 | tf_op jit(solution)/shard_map/dot_general | solution.py:41
  708.2 22.6 %convolution_convert_fusion.2 = bf16[2048,2048]{1,0:T(8,128)(2,1)S(1)} fusion(bf16[2048,2048]{1,0:T(8,128)(2,1)} %bitcast.83, bf16[2048,1024]{0,1:T(8,128)(2,1)} %get-tuple-element.78, bf16[2048,1024]{0,1:T(8,128)(2,1)} %get-tuple-element.77), kind=kOutput, calls=%fused_computation.16 | convolution fusion | flops 17200840704 | bytes 25165824 | tf_op jit(solution)/shard_map/dot_general | solution.py:41
  754.2 26.1 %convolution_convert_fusion = bf16[2048,2048]{1,0:T(8,128)(2,1)} fusion(bf16[2048,1024]{0,1:T(8,128)(2,1)} %get-tuple-element.78, bf16[2048,1024]{0,1:T(8,128)(2,1)} %get-tuple-element.77, bf16[512,2048]{1,0:T(8,128)(2,1)} %copy-done.113, bf16[512,2048]{1,0:T(8,128)(2,1)} %copy-done.111, bf16[512,2048]{1,0:T(8,128)(2,1)} %copy-done.112, ...), kind=kOutput, calls=%fused_computation.14 | convolution fusion | flops 17234395136 | bytes 25165824 | tf_op jit(solution)/shard_map/dot_general | solution.py:41
  812.1 21.9 %collective-permute-done.105 = bf16[256,2048]{1,0:T(8,128)(2,1)} collective-permute-done((bf16[256,2048]{1,0:T(8,128)(2,1)}, bf16[256,2048]{1,0:T(8,128)(2,1)}, u32[]{:S(2)}, u32[]{:S(2)}) %collective-permute-start.105) | collective-permute-done | bytes 1048608 | tf_op jit(solution)/shard_map/ppermute | solution.py:56
  834.5 21.9 %collective-permute-done.107 = bf16[256,2048]{1,0:T(8,128)(2,1)} collective-permute-done((bf16[256,2048]{1,0:T(8,128)(2,1)}, bf16[256,2048]{1,0:T(8,128)(2,1)}, u32[]{:S(2)}, u32[]{:S(2)}) %collective-permute-start.107) | collective-permute-done | bytes 1048608 | tf_op jit(solution)/shard_map/ppermute | solution.py:56
  874.7 35.5 %collective-permute-done.114 = bf16[128,2048]{1,0:T(8,128)(2,1)S(1)} collective-permute-done((bf16[128,2048]{1,0:T(8,128)(2,1)S(1)}, bf16[128,2048]{1,0:T(8,128)(2,1)S(1)}, u32[]{:S(2)}, u32[]{:S(2)}) %collective-permute-start.114) | collective-permute-done | bytes 524320 | tf_op jit(solution)/shard_map/ppermute | solution.py:56
  919.8 47.3 %collective-permute-done.116 = bf16[128,2048]{1,0:T(8,128)(2,1)S(1)} collective-permute-done((bf16[128,2048]{1,0:T(8,128)(2,1)S(1)}, bf16[128,2048]{1,0:T(8,128)(2,1)S(1)}, u32[]{:S(2)}, u32[]{:S(2)}) %collective-permute-start.116) | collective-permute-done | bytes 524320 | tf_op jit(solution)/shard_map/ppermute | solution.py:56
  967.7 22.0 %collective-permute-start.118 = (bf16[128,2048]{1,0:T(8,128)(2,1)S(1)}, bf16[128,2048]{1,0:T(8,128)(2,1)S(1)}, u32[]{:S(2)}, u32[]{:S(2)}) collective-permute-start(bf16[128,2048]{1,0:T(8,128)(2,1)S(1)} %get-tuple-element.111), channel_id=1, source_target_pairs={{8,0},{12,4},{16,8},{20,12},{24,16},{28,20},{0,24},{4,28},{9,1},{1... | collective-permute-start | bytes 1572872 | tf_op jit(solution)/shard_map/ppermute | solution.py:56
  1007.7 80.0 %collective-permute-done.110 = bf16[64,2048]{1,0:T(8,128)(2,1)S(1)} collective-permute-done((bf16[64,2048]{1,0:T(8,128)(2,1)S(1)}, bf16[64,2048]{1,0:T(8,128)(2,1)S(1)}, u32[]{:S(2)}, u32[]{:S(2)}) %collective-permute-start.110) | collective-permute-done | bytes 262176 | tf_op jit(solution)/shard_map/ppermute | solution.py:46
  1115.5 36.5 %collective-permute-done.67 = bf16[512,2048]{1,0:T(8,128)(2,1)} collective-permute-done((bf16[512,2048]{1,0:T(8,128)(2,1)}, bf16[512,2048]{1,0:T(8,128)(2,1)}, u32[]{:S(2)}, u32[]{:S(2)}) %collective-permute-start.67) | collective-permute-done | bytes 2097184 | tf_op jit(solution)/shard_map/ppermute | solution.py:46
  1191.3 28.2 %attend_back.1 = (f32[2048,256]{1,0:T(8,128)}, f32[2048,256]{1,0:T(8,128)}, f32[2048,256]{1,0:T(8,128)}) custom-call(bf16[2048,256]{1,0:T(8,128)(2,1)S(1)} %copy-done.5, bf16[2048,256]{1,0:T(8,128)(2,1)S(1)} %copy-done.11, bf16[2048,256]{1,0:T(8,128)(2,1)S(1)} %copy-done.9, f32[2048,128]{1,0:T(8,128)S(1)} %copy-done.7, f32[8,2048]{1,0:T(8,128)S(1)} %copy-done.13, ...), custom_call_target="tpu_custom_call" | custom-call | flops 6710886400 | bytes 12582912 | tf_op jit(solution)/shard_map/attend_back/pallas_call | solution.py:267
  1241.0 33.3 %state_scan_back.1 = (f32[2048,768]{1,0:T(8,128)}, f32[2048,256]{1,0:T(8,128)S(1)}, f32[2048,256]{1,0:T(8,128)}, f32[2048,128]{1,0:T(8,128)S(1)}, f32[8,8,768]{2,1,0:T(8,128)S(1)}) custom-call(f32[2048,1792]{1,0:T(8,128)} %fusion.115.x_ref, f32[2048,1152]{1,0:T(8,128)} %copy.197.k_ref.r_ref, f32[2048,1152]{1,0:T(8,128)} %copy.197.k_ref.r_ref, ...), custom_call_target="tpu_custom_call" | custom-call | flops 8053063680 | bytes 37748736 | tf_op jit(solution)/shard_map/state_scan_back/pallas_call | solution.py:467
  1285.6 19.0 %fusion.118 = f32[2048,2048]{1,0:T(8,128)} fusion(bf16[2048,1152]{1,0:T(8,128)(2,1)S(1)} %pad_dynamic-update-slice_fusion, bf16[2048,1152]{1,0:T(8,128)(2,1)} %bitcast.40), kind=kOutput, calls=%fused_computation.359 | convolution fusion | flops 9663676416 | bytes 26214400 | tf_op jit(solution)/shard_map/dot_general | solution.py:41
  1307.7 22.6 %add_convert_fusion = bf16[2048,2048]{1,0:T(8,128)(2,1)} fusion(f32[2048,2048]{1,0:T(8,128)} %fusion.118, bf16[2048,1792]{1,0:T(8,128)(2,1)} %bitcast.512, bf16[2048,256]{1,0:T(8,128)(2,1)} %convert_element_type.589, bf16[2048,768]{1,0:T(8,128)(2,1)} %convert_element_type.588, bf16[2048,768]{1,0:T(8,128)(2,1)S(1)} %copy-done.46), kind=kOutput, calls=%fused_computation.3 | convolution fusion | flops 15062794240 | bytes 39845888 | tf_op jit(solution)/shard_map/dot_general | solution.py:41
  1330.2 20.4 %convolution_convert_fusion.5 = bf16[2048,1792]{1,0:T(8,128)(2,1)S(1)} fusion(bf16[2048,2048]{1,0:T(8,128)(2,1)} %fusion.1, bf16[2048,256]{1,0:T(8,128)(2,1)} %convert_element_type.589, bf16[2048,768]{1,0:T(8,128)(2,1)} %convert_element_type.588, bf16[2048,768]{1,0:T(8,128)(2,1)} %get-tuple-element.75), kind=kOutput, calls=%fused_computation.19 | convolution fusion | flops 15058075648 | bytes 23068672 | tf_op jit(solution)/shard_map/dot_general | solution.py:41
  1395.8 19.7 %collective-permute-done.80 = bf16[256,1792]{1,0:T(8,128)(2,1)} collective-permute-done((bf16[256,1792]{1,0:T(8,128)(2,1)}, bf16[256,1792]{1,0:T(8,128)(2,1)}, u32[]{:S(2)}, u32[]{:S(2)}) %collective-permute-start.80) | collective-permute-done | bytes 917536 | tf_op jit(solution)/shard_map/ppermute | solution.py:56
  1427.8 36.0 %collective-permute-done.97 = bf16[128,2048]{1,0:T(8,128)(2,1)S(1)} collective-permute-done((bf16[128,2048]{1,0:T(8,128)(2,1)S(1)}, bf16[128,2048]{1,0:T(8,128)(2,1)S(1)}, u32[]{:S(2)}, u32[]{:S(2)}) %collective-permute-start.97) | collective-permute-done | bytes 524320 | tf_op jit(solution)/shard_map/ppermute | solution.py:56
  1468.4 18.0 %collective-permute-done.77 = bf16[256,1792]{1,0:T(8,128)(2,1)S(1)} collective-permute-done((bf16[256,1792]{1,0:T(8,128)(2,1)S(1)}, bf16[256,1792]{1,0:T(8,128)(2,1)S(1)}, u32[]{:S(2)}, u32[]{:S(2)}) %collective-permute-start.77) | collective-permute-done | bytes 917536 | tf_op jit(solution)/shard_map/ppermute | solution.py:56
  1499.7 30.9 %collective-permute-done.83 = bf16[64,1792]{1,0:T(8,128)(2,1)S(1)} collective-permute-done((bf16[64,1792]{1,0:T(8,128)(2,1)S(1)}, bf16[64,1792]{1,0:T(8,128)(2,1)S(1)}, u32[]{:S(2)}, u32[]{:S(2)}) %collective-permute-start.83) | collective-permute-done | bytes 229408 | tf_op jit(solution)/shard_map/ppermute | solution.py:46
  1586.4 34.0 %collective-permute-done.74 = bf16[512,2048]{1,0:T(8,128)(2,1)} collective-permute-done((bf16[512,2048]{1,0:T(8,128)(2,1)}, bf16[512,2048]{1,0:T(8,128)(2,1)}, u32[]{:S(2)}, u32[]{:S(2)}) %collective-permute-start.74) | collective-permute-done | bytes 2097184 | tf_op jit(solution)/shard_map/ppermute | solution.py:46
  1625.3 37.0 %psum.7 = f32[7312]{0:T(1024)S(1)} all-reduce(f32[7312]{0:T(1024)S(1)} %concatenate.63), channel_id=1, replica_groups=mesh['dp'=8,'ctx'=4] {'dp','ctx'}, use_global_device_ids=true, to_apply=%region_14.15 | all-reduce | flops 7312 | bytes 58496 | tf_op jit(solution)/shard_map/psum | solution.py:815
  (773 shorter events, 754.0 us)
Async XLA Ops:
  44.1 256.2 %collective-permute-start = (bf16[512,2048]{1,0:T(8,128)(2,1)S(1)}, bf16[512,2048]{1,0:T(8,128)(2,1)}, u32[]{:S(2)}, u32[]{:S(2)}) collective-permute-start(bf16[512,2048]{1,0:T(8,128)(2,1)S(1)} %bitcast.488), channel_id=1, source_target_pairs={{2,0},{3,1},{0,2},{1,3},{6,4},{7,5},{4,6},{5,7},{10,8},{11,9},{8,1... | collective-permute-start | bytes 6291464 | tf_op jit(solution)/shard_map/ppermute | solution.py:46
  45.9 259.7 %collective-permute-start.1 = (bf16[512,2048]{1,0:T(8,128)(2,1)S(1)}, bf16[512,2048]{1,0:T(8,128)(2,1)S(1)}, u32[]{:S(2)}, u32[]{:S(2)}) collective-permute-start(bf16[512,2048]{1,0:T(8,128)(2,1)S(1)} %bitcast.489), channel_id=1, source_target_pairs={{1,0},{0,1},{3,2},{2,3},{5,4},{4,5},{7,6},{6,7},{9,8},{8,9},{11,10... | collective-permute-start | bytes 6291464 | tf_op jit(solution)/shard_map/ppermute | solution.py:46
  46.9 78.6 %collective-permute-start.28 = (bf16[128,2048]{1,0:T(8,128)(2,1)}, bf16[128,2048]{1,0:T(8,128)(2,1)S(1)}, u32[]{:S(2)}, u32[]{:S(2)}) collective-permute-start(bf16[128,2048]{1,0:T(8,128)(2,1)} %get-tuple-element.74), channel_id=1, source_target_pairs={{16,0},{20,4},{24,8},{28,12},{0,16},{4,20},{8,24},{12,28},{17,1},{... | collective-permute-start | bytes 1572872 | tf_op jit(solution)/shard_map/ppermute | solution.py:56
  48.9 77.2 %collective-permute-start.29 = (bf16[128,2048]{1,0:T(8,128)(2,1)}, bf16[128,2048]{1,0:T(8,128)(2,1)S(1)}, u32[]{:S(2)}, u32[]{:S(2)}) collective-permute-start(bf16[128,2048]{1,0:T(8,128)(2,1)} %get-tuple-element.74), channel_id=1, source_target_pairs={{8,0},{12,4},{16,8},{20,12},{24,16},{28,20},{0,24},{4,28},{9,1},{1... | collective-permute-start | bytes 1572872 | tf_op jit(solution)/shard_map/ppermute | solution.py:56
  213.3 270.0 %collective-permute-start.51 = (bf16[128,2048]{1,0:T(8,128)(2,1)}, bf16[128,2048]{1,0:T(8,128)(2,1)}, u32[]{:S(2)}, u32[]{:S(2)}) collective-permute-start(bf16[128,2048]{1,0:T(8,128)(2,1)} %get-tuple-element.68), channel_id=1, source_target_pairs={{16,0},{20,4},{24,8},{28,12},{0,16},{4,20},{8,24},{12,28},{17,1},{... | collective-permute-start | bytes 1572872 | tf_op jit(solution)/shard_map/ppermute | solution.py:56
  282.1 203.5 %collective-permute-start.52 = (bf16[128,2048]{1,0:T(8,128)(2,1)}, bf16[128,2048]{1,0:T(8,128)(2,1)}, u32[]{:S(2)}, u32[]{:S(2)}) collective-permute-start(bf16[128,2048]{1,0:T(8,128)(2,1)} %get-tuple-element.68), channel_id=1, source_target_pairs={{8,0},{12,4},{16,8},{20,12},{24,16},{28,20},{0,24},{4,28},{9,1},{1... | collective-permute-start | bytes 1572872 | tf_op jit(solution)/shard_map/ppermute | solution.py:56
  305.7 181.8 %collective-permute-start.53 = (bf16[128,2048]{1,0:T(8,128)(2,1)}, bf16[128,2048]{1,0:T(8,128)(2,1)}, u32[]{:S(2)}, u32[]{:S(2)}) collective-permute-start(bf16[128,2048]{1,0:T(8,128)(2,1)} %get-tuple-element.68), channel_id=1, source_target_pairs={{24,0},{28,4},{0,8},{4,12},{8,16},{12,20},{16,24},{20,28},{25,1},{... | collective-permute-start | bytes 1572872 | tf_op jit(solution)/shard_map/ppermute | solution.py:56
  485.6 71.7 %collective-permute-start.44 = (bf16[256,2048]{1,0:T(8,128)(2,1)S(1)}, bf16[256,2048]{1,0:T(8,128)(2,1)S(1)}, u32[]{:S(2)}, u32[]{:S(2)}) collective-permute-start(bf16[256,2048]{1,0:T(8,128)(2,1)S(1)} %bitcast.524), channel_id=1, source_target_pairs={{16,0},{20,4},{24,8},{28,12},{0,16},{4,20},{8,24},{12,28},{17,1},{... | collective-permute-start | bytes 3145736 | tf_op jit(solution)/shard_map/ppermute | solution.py:56
  487.5 70.9 %collective-permute-start.45 = (bf16[256,2048]{1,0:T(8,128)(2,1)S(1)}, bf16[256,2048]{1,0:T(8,128)(2,1)S(1)}, u32[]{:S(2)}, u32[]{:S(2)}) collective-permute-start(bf16[256,2048]{1,0:T(8,128)(2,1)S(1)} %bitcast.525), channel_id=1, source_target_pairs={{8,0},{12,4},{16,8},{20,12},{24,16},{28,20},{0,24},{4,28},{9,1},{1... | collective-permute-start | bytes 3145736 | tf_op jit(solution)/shard_map/ppermute | solution.py:56
  497.4 62.6 %collective-permute-start.46 = (bf16[256,2048]{1,0:T(8,128)(2,1)S(1)}, bf16[256,2048]{1,0:T(8,128)(2,1)S(1)}, u32[]{:S(2)}, u32[]{:S(2)}) collective-permute-start(bf16[256,2048]{1,0:T(8,128)(2,1)S(1)} %bitcast.526), channel_id=1, source_target_pairs={{24,0},{28,4},{0,8},{4,12},{8,16},{12,20},{16,24},{20,28},{25,1},{... | collective-permute-start | bytes 3145736 | tf_op jit(solution)/shard_map/ppermute | solution.py:56
  557.3 72.5 %collective-permute-start.62 = (bf16[512,2048]{1,0:T(8,128)(2,1)S(1)}, bf16[512,2048]{1,0:T(8,128)(2,1)}, u32[]{:S(2)}, u32[]{:S(2)}) collective-permute-start(bf16[512,2048]{1,0:T(8,128)(2,1)S(1)} %bitcast.541), channel_id=1, source_target_pairs={{2,0},{3,1},{0,2},{1,3},{6,4},{7,5},{4,6},{5,7},{10,8},{11,9},{8,1... | collective-permute-start | bytes 6291464 | tf_op jit(solution)/shard_map/ppermute | solution.py:46
  560.0 69.8 %collective-permute-start.49 = (bf16[256,2048]{1,0:T(8,128)(2,1)S(1)}, bf16[256,2048]{1,0:T(8,128)(2,1)S(1)}, u32[]{:S(2)}, u32[]{:S(2)}) collective-permute-start(bf16[256,2048]{1,0:T(8,128)(2,1)S(1)} %collective-permute-done.46), channel_id=1, source_target_pairs={{4,0},{0,4},{12,8},{8,12},{20,16},{16,20},{28,24},{24,28},{5,1},{1... | collective-permute-start | bytes 3145736 | tf_op jit(solution)/shard_map/ppermute | solution.py:56
  575.7 66.9 %collective-permute-start.38 = (bf16[512,2048]{1,0:T(8,128)(2,1)S(1)}, bf16[512,2048]{1,0:T(8,128)(2,1)S(1)}, u32[]{:S(2)}, u32[]{:S(2)}) collective-permute-start(bf16[512,2048]{1,0:T(8,128)(2,1)S(1)} %multiply_convert_fusion.6), channel_id=1, source_target_pairs={{1,0},{0,1},{3,2},{2,3},{5,4},{4,5},{7,6},{6,7},{9,8},{8,9},{11,10... | collective-permute-start | bytes 6291464 | tf_op jit(solution)/shard_map/ppermute | solution.py:46
  708.2 202.0 %collective-permute-start.59 = (bf16[512,2048]{1,0:T(8,128)(2,1)}, bf16[512,2048]{1,0:T(8,128)(2,1)}, u32[]{:S(2)}, u32[]{:S(2)}) collective-permute-start(bf16[512,2048]{1,0:T(8,128)(2,1)} %get-tuple-element.92), channel_id=1, source_target_pairs={{1,0},{0,1},{3,2},{2,3},{5,4},{4,5},{7,6},{6,7},{9,8},{8,9},{11,10... | collective-permute-start | bytes 6291464 | tf_op jit(solution)/shard_map/ppermute | solution.py:46
  735.4 181.7 %collective-permute-start.65 = (bf16[512,2048]{1,0:T(8,128)(2,1)}, bf16[512,2048]{1,0:T(8,128)(2,1)}, u32[]{:S(2)}, u32[]{:S(2)}) collective-permute-start(bf16[512,2048]{1,0:T(8,128)(2,1)} %get-tuple-element.90), channel_id=1, source_target_pairs={{1,0},{0,1},{3,2},{2,3},{5,4},{4,5},{7,6},{6,7},{9,8},{8,9},{11,10... | collective-permute-start | bytes 6291464 | tf_op jit(solution)/shard_map/ppermute | solution.py:46
  789.1 67.4 %collective-permute-start.107 = (bf16[256,2048]{1,0:T(8,128)(2,1)}, bf16[256,2048]{1,0:T(8,128)(2,1)}, u32[]{:S(2)}, u32[]{:S(2)}) collective-permute-start(bf16[256,2048]{1,0:T(8,128)(2,1)} %get-tuple-element.81), channel_id=1, source_target_pairs={{4,0},{0,4},{12,8},{8,12},{20,16},{16,20},{28,24},{24,28},{5,1},{1... | collective-permute-start | bytes 3145736 | tf_op jit(solution)/shard_map/ppermute | solution.py:56
  834.0 133.2 %collective-permute-start.102 = (bf16[256,2048]{1,0:T(8,128)(2,1)S(1)}, bf16[256,2048]{1,0:T(8,128)(2,1)S(1)}, u32[]{:S(2)}, u32[]{:S(2)}) collective-permute-start(bf16[256,2048]{1,0:T(8,128)(2,1)S(1)} %get-tuple-element.80), channel_id=1, source_target_pairs={{4,0},{0,4},{12,8},{8,12},{20,16},{16,20},{28,24},{24,28},{5,1},{1... | collective-permute-start | bytes 3145736 | tf_op jit(solution)/shard_map/ppermute | solution.py:56
  867.9 99.8 %collective-permute-start.104 = (bf16[256,2048]{1,0:T(8,128)(2,1)S(1)}, bf16[256,2048]{1,0:T(8,128)(2,1)S(1)}, u32[]{:S(2)}, u32[]{:S(2)}) collective-permute-start(bf16[256,2048]{1,0:T(8,128)(2,1)S(1)} %get-tuple-element.84), channel_id=1, source_target_pairs={{16,0},{20,4},{24,8},{28,12},{0,16},{4,20},{8,24},{12,28},{17,1},{... | collective-permute-start | bytes 3145736 | tf_op jit(solution)/shard_map/ppermute | solution.py:56
  910.2 79.6 %collective-permute-start.106 = (bf16[256,2048]{1,0:T(8,128)(2,1)S(1)}, bf16[256,2048]{1,0:T(8,128)(2,1)S(1)}, u32[]{:S(2)}, u32[]{:S(2)}) collective-permute-start(bf16[256,2048]{1,0:T(8,128)(2,1)S(1)} %get-tuple-element.86), channel_id=1, source_target_pairs={{24,0},{28,4},{0,8},{4,12},{8,16},{12,20},{16,24},{20,28},{25,1},{... | collective-permute-start | bytes 3145736 | tf_op jit(solution)/shard_map/ppermute | solution.py:56
  910.2 80.8 %collective-permute-start.108 = (bf16[256,2048]{1,0:T(8,128)(2,1)S(1)}, bf16[256,2048]{1,0:T(8,128)(2,1)S(1)}, u32[]{:S(2)}, u32[]{:S(2)}) collective-permute-start(bf16[256,2048]{1,0:T(8,128)(2,1)S(1)} %get-tuple-element.85), channel_id=1, source_target_pairs={{8,0},{12,4},{16,8},{20,12},{24,16},{28,20},{0,24},{4,28},{9,1},{1... | collective-permute-start | bytes 3145736 | tf_op jit(solution)/shard_map/ppermute | solution.py:56
  967.2 120.5 %collective-permute-start.58 = (bf16[512,2048]{1,0:T(8,128)(2,1)S(1)}, bf16[512,2048]{1,0:T(8,128)(2,1)S(1)}, u32[]{:S(2)}, u32[]{:S(2)}) collective-permute-start(bf16[512,2048]{1,0:T(8,128)(2,1)S(1)} %copy-done.58), channel_id=1, source_target_pairs={{1,0},{0,1},{3,2},{2,3},{5,4},{4,5},{7,6},{6,7},{9,8},{8,9},{11,10... | collective-permute-start | bytes 6291464 | tf_op jit(solution)/shard_map/ppermute | solution.py:46
  967.2 120.5 %collective-permute-start.64 = (bf16[512,2048]{1,0:T(8,128)(2,1)S(1)}, bf16[512,2048]{1,0:T(8,128)(2,1)S(1)}, u32[]{:S(2)}, u32[]{:S(2)}) collective-permute-start(bf16[512,2048]{1,0:T(8,128)(2,1)S(1)} %copy-done.59), channel_id=1, source_target_pairs={{1,0},{0,1},{3,2},{2,3},{5,4},{4,5},{7,6},{6,7},{9,8},{8,9},{11,10... | collective-permute-start | bytes 6291464 | tf_op jit(solution)/shard_map/ppermute | solution.py:46
  989.8 98.0 %collective-permute-start.60 = (bf16[512,2048]{1,0:T(8,128)(2,1)S(1)}, bf16[512,2048]{1,0:T(8,128)(2,1)S(1)}, u32[]{:S(2)}, u32[]{:S(2)}) collective-permute-start(bf16[512,2048]{1,0:T(8,128)(2,1)S(1)} %add_convert_fusion.3), channel_id=1, source_target_pairs={{2,0},{3,1},{0,2},{1,3},{6,4},{7,5},{4,6},{5,7},{10,8},{11,9},{8,1... | collective-permute-start | bytes 6291464 | tf_op jit(solution)/shard_map/ppermute | solution.py:46
  991.0 96.7 %collective-permute-start.66 = (bf16[512,2048]{1,0:T(8,128)(2,1)S(1)}, bf16[512,2048]{1,0:T(8,128)(2,1)S(1)}, u32[]{:S(2)}, u32[]{:S(2)}) collective-permute-start(bf16[512,2048]{1,0:T(8,128)(2,1)S(1)} %add_convert_fusion.1), channel_id=1, source_target_pairs={{2,0},{3,1},{0,2},{1,3},{6,4},{7,5},{4,6},{5,7},{10,8},{11,9},{8,1... | collective-permute-start | bytes 6291464 | tf_op jit(solution)/shard_map/ppermute | solution.py:46
  1006.4 81.3 %collective-permute-start.110 = (bf16[64,2048]{1,0:T(8,128)(2,1)S(1)}, bf16[64,2048]{1,0:T(8,128)(2,1)S(1)}, u32[]{:S(2)}, u32[]{:S(2)}) collective-permute-start(bf16[64,2048]{1,0:T(8,128)(2,1)S(1)} %get-tuple-element.136), channel_id=1, source_target_pairs={{2,0},{3,1},{0,2},{1,3},{6,4},{7,5},{4,6},{5,7},{10,8},{11,9},{8,1... | collective-permute-start | bytes 786440 | tf_op jit(solution)/shard_map/ppermute | solution.py:46
  1223.5 131.1 %collective-permute-start.100 = (bf16[128,2048]{1,0:T(8,128)(2,1)}, bf16[128,2048]{1,0:T(8,128)(2,1)}, u32[]{:S(2)}, u32[]{:S(2)}) collective-permute-start(bf16[128,2048]{1,0:T(8,128)(2,1)} %get-tuple-element.114), channel_id=1, source_target_pairs={{4,0},{0,4},{12,8},{8,12},{20,16},{16,20},{28,24},{24,28},{5,1},{1... | collective-permute-start | bytes 1572872 | tf_op jit(solution)/shard_map/ppermute | solution.py:56
  1225.0 152.8 %collective-permute-start.96 = (bf16[128,2048]{1,0:T(8,128)(2,1)}, bf16[128,2048]{1,0:T(8,128)(2,1)}, u32[]{:S(2)}, u32[]{:S(2)}) collective-permute-start(bf16[128,2048]{1,0:T(8,128)(2,1)} %get-tuple-element.116), channel_id=1, source_target_pairs={{4,0},{0,4},{12,8},{8,12},{20,16},{16,20},{28,24},{24,28},{5,1},{1... | collective-permute-start | bytes 1572872 | tf_op jit(solution)/shard_map/ppermute | solution.py:56
  1225.5 152.8 %collective-permute-start.98 = (bf16[128,2048]{1,0:T(8,128)(2,1)}, bf16[128,2048]{1,0:T(8,128)(2,1)}, u32[]{:S(2)}, u32[]{:S(2)}) collective-permute-start(bf16[128,2048]{1,0:T(8,128)(2,1)} %get-tuple-element.115), channel_id=1, source_target_pairs={{4,0},{0,4},{12,8},{8,12},{20,16},{16,20},{28,24},{24,28},{5,1},{1... | collective-permute-start | bytes 1572872 | tf_op jit(solution)/shard_map/ppermute | solution.py:56
  1378.3 89.7 %collective-permute-start.75 = (bf16[256,1792]{1,0:T(8,128)(2,1)S(1)}, bf16[256,1792]{1,0:T(8,128)(2,1)S(1)}, u32[]{:S(2)}, u32[]{:S(2)}) collective-permute-start(bf16[256,1792]{1,0:T(8,128)(2,1)S(1)} %copy-done.67), channel_id=1, source_target_pairs={{4,0},{0,4},{12,8},{8,12},{20,16},{16,20},{28,24},{24,28},{5,1},{1... | collective-permute-start | bytes 2752520 | tf_op jit(solution)/shard_map/ppermute | solution.py:56
  1395.8 67.9 %collective-permute-start.97 = (bf16[128,2048]{1,0:T(8,128)(2,1)S(1)}, bf16[128,2048]{1,0:T(8,128)(2,1)S(1)}, u32[]{:S(2)}, u32[]{:S(2)}) collective-permute-start(bf16[128,2048]{1,0:T(8,128)(2,1)S(1)} %get-tuple-element.117), channel_id=1, source_target_pairs={{16,0},{20,4},{24,8},{28,12},{0,16},{4,20},{8,24},{12,28},{17,1},{... | collective-permute-start | bytes 1572872 | tf_op jit(solution)/shard_map/ppermute | solution.py:56
  1467.9 98.0 %collective-permute-start.73 = (bf16[512,2048]{1,0:T(8,128)(2,1)}, bf16[512,2048]{1,0:T(8,128)(2,1)}, u32[]{:S(2)}, u32[]{:S(2)}) collective-permute-start(bf16[512,2048]{1,0:T(8,128)(2,1)} %get-tuple-element.88), channel_id=1, source_target_pairs={{1,0},{0,1},{3,2},{2,3},{5,4},{4,5},{7,6},{6,7},{9,8},{8,9},{11,10... | collective-permute-start | bytes 6291464 | tf_op jit(solution)/shard_map/ppermute | solution.py:46
  1486.4 100.0 %collective-permute-start.72 = (bf16[512,2048]{1,0:T(8,128)(2,1)}, bf16[512,2048]{1,0:T(8,128)(2,1)}, u32[]{:S(2)}, u32[]{:S(2)}) collective-permute-start(bf16[512,2048]{1,0:T(8,128)(2,1)} %get-tuple-element.87), channel_id=1, source_target_pairs={{1,0},{0,1},{3,2},{2,3},{5,4},{4,5},{7,6},{6,7},{9,8},{8,9},{11,10... | collective-permute-start | bytes 6291464 | tf_op jit(solution)/shard_map/ppermute | solution.py:46
  (213 other events, 6301.9 us)
